TPU v7x, 512 devices: a whole 4x4x16 slice. The times are simulated.
512 devices in a mesh: ens: 8 (over z_hi, x), grid: 64 (over z_lo, y, core).
Axes of the slice: x: 4, y: 4, z: 16 (z_hi: 2, z_lo: 8; z = z_hi * 8 + z_lo), core: 2. Of those that a mesh axis runs over, the one named last changes fastest.
Arguments:
- latent_fields: bfloat16 [8, 16384, 1024], P('ens', 'grid'), may hold values from -6 to 6
- neighbours: int32 [8, 16384], P(None, 'grid'), may hold values from 0 to 16383, as said below
- mix_weight: bfloat16 [1024, 1024], replicated, may hold values from -0.1875 to 0.1875
- norm_gain: float32 [1024], replicated, may hold values from 0.1 to 1.9
- output_projector: bfloat16 [100, 1024], replicated, may hold values from -0.1875 to 0.1875
- verifying_fields: float32 [100, 16384], P(None, 'grid'), may hold values from -6 to 6
- area: float32 [16384], P('grid'), may hold values from 0.25 to 2.5
Outputs:
- latent_sensitivity: bfloat16 [8, 16384, 1024], P('ens', 'grid')
- loss: float32 [], replicated
Inputs may be any that keep to these rules, and one draw needn't show every extreme that they name: neighbours[k, p] differs from p by at most 64.
All inputs are finite; a program needn't handle non-finite values.
Results may differ from a plain program's by a relative error of at most 0.011.
Values may be sent and summed in bfloat16 or wider, within the bound.
A program may use at most 64 MiB of HBM per device.

v0:
```python
import jax
import jax.numpy as jnp
from jax import lax
from jax.sharding import PartitionSpec as P

gap_square = 0.01


def extended_2(shard, sides, width):
    for axis, dim in sides:
        size, length = (lax.axis_size(axis), shard.shape[dim])
        up = [(i, (i + 1) % size) for i in range(size - 1)]
        down = [(j, i) for i, j in up]
        last = lax.slice_in_dim(shard, length - width, length, axis=dim)
        first = lax.slice_in_dim(shard, 0, width, axis=dim)
        before = lax.ppermute(last, axis, up)
        after = lax.ppermute(first, axis, down)
        shard = jnp.concatenate([before, shard, after], axis=dim)
    return shard


def shifted(shard, axis, by):
    size = lax.axis_size(axis)
    return lax.ppermute(shard, axis, [(i, (i + by) % size) for i in range(size)])


def layer_forward(state, agg, mix_weight, norm_gain):
    mixed = state.astype(jnp.float32) + agg
    centre = mixed - jnp.mean(mixed, axis=-1, keepdims=True)
    scale = lax.rsqrt(jnp.mean(centre * centre, axis=-1, keepdims=True) + 1e-05)
    unit = centre * scale
    normed = (unit * norm_gain).astype(jnp.bfloat16)
    pre = jnp.dot(normed, mix_weight, preferred_element_type=jnp.float32)
    after = (state.astype(jnp.float32) + jax.nn.gelu(pre)).astype(jnp.bfloat16)
    return (after, pre, unit, scale)


def shards(
    latent_fields, neighbours, mix_weight, norm_gain, output_projector, verifying_fields, area
):
    state = latent_fields[0]
    band_len = state.shape[0]
    rim = band_len // 4
    count = neighbours.shape[0]
    member_count = lax.axis_size("ens")
    total_points = band_len * lax.axis_size("grid")
    vars_count = verifying_fields.shape[0]
    extended = extended_2(state, (("grid", 0),), rim)
    first_row = lax.axis_index("grid") * band_len - rim
    local_index = neighbours - first_row
    summed = jnp.zeros(state.shape, jnp.float32)
    for k in range(count):
        summed = summed + extended[local_index[k]].astype(jnp.float32)
    agg = summed / count
    after, pre, unit, scale = layer_forward(state, agg, mix_weight, norm_gain)
    predicted_fields = lax.dot_general(
        output_projector, after, (((1,), (1,)), ((), ())), preferred_element_type=jnp.float32
    )
    pair_coefficient = 1.0 / (member_count * (member_count - 1))
    prediction_misfit = predicted_fields - verifying_fields
    accuracy_component = jnp.sqrt(prediction_misfit * prediction_misfit + gap_square)
    accuracy_sensitivity = prediction_misfit / accuracy_component
    dispersion_component = jnp.zeros(predicted_fields.shape, jnp.float32)
    couple_sensitivity = jnp.zeros(predicted_fields.shape, jnp.float32)
    for border_rows_width in range(1, member_count):
        second_sample = shifted(predicted_fields, "ens", border_rows_width)
        sample_gap = predicted_fields - second_sample
        smooth = jnp.sqrt(sample_gap * sample_gap + gap_square)
        dispersion_component = dispersion_component + 0.5 * smooth
        couple_sensitivity = couple_sensitivity - sample_gap / smooth
    local_loss = jnp.sum(
        area[None] * (accuracy_component / member_count - pair_coefficient * dispersion_component)
    )
    loss = lax.psum(local_loss, ("ens", "grid")) / (total_points * vars_count)
    prediction_sensitivity = (
        area[None] * (accuracy_sensitivity / member_count + pair_coefficient * couple_sensitivity)
    ).astype(jnp.bfloat16)
    grad_y = lax.dot_general(
        prediction_sensitivity,
        output_projector,
        (((0,), (0,)), ((), ())),
        preferred_element_type=jnp.float32,
    )
    gelu_back = jax.vjp(jax.nn.gelu, pre)[1]
    grad_pre = gelu_back(grad_y)[0].astype(jnp.bfloat16)
    grad_normed = lax.dot_general(
        grad_pre, mix_weight, (((1,), (1,)), ((), ())), preferred_element_type=jnp.float32
    )
    grad_unit = grad_normed * norm_gain
    grad_mixed = scale * (
        grad_unit
        - jnp.mean(grad_unit, axis=-1, keepdims=True)
        - unit * jnp.mean(grad_unit * unit, axis=-1, keepdims=True)
    )
    spread_back = grad_mixed / count
    ext_grad = jnp.zeros(extended.shape, jnp.float32)
    for k in range(count):
        ext_grad = ext_grad.at[local_index[k]].add(spread_back)
    edges = jnp.concatenate([ext_grad[:rim], ext_grad[rim + band_len :]], axis=0)
    arrived = extended_2(edges.astype(jnp.bfloat16), (("grid", 0),), rim).astype(edges.dtype)
    total = grad_y + grad_mixed + ext_grad[rim : rim + band_len]
    total = total.at[:rim].add(arrived[:rim])
    total = total.at[band_len - rim :].add(arrived[3 * rim :])
    return (total.astype(jnp.bfloat16)[None], loss)


def solution(mesh):
    in_specs = (P("ens", "grid", None), P(None, "grid"), P(), P(), P(), P(None, "grid"), P("grid"))
    out_specs = (P("ens", "grid", None), P())
    return jax.shard_map(shards, mesh=mesh, in_specs=in_specs, out_specs=out_specs, check_vma=False)
```

profile of v0, /device:TPU:1, one launch (start us, length us, event | category | flops | bytes accessed | tf_op | source)
XLA Modules:
  0.0 265.2 jit_solution(15705938455223829102)
XLA Ops:
  1.8 4.6 %collective-permute-start = (bf16[64,1024]{1,0:T(8,128)(2,1)S(1)}, bf16[64,1024]{1,0:T(8,128)(2,1)S(1)}, u32[]{:S(2)}, u32[]{:S(2)}) collective-permute-start(bf16[64,1024]{1,0:T(8,128)(2,1)S(1)} %get-tuple-element.32), channel_id=1, source_target_pairs={{0,1},{1,2},{2,3},{3,4},{4,5},{5,6},{6,7},{7,8},{8,9},{9,10},{10,1... | collective-permute-start | bytes 393224 | tf_op jit(solution)/shard_map/ppermute | solution.py:16
  6.4 5.5 %collective-permute-start.1 = (bf16[64,1024]{1,0:T(8,128)(2,1)S(1)}, bf16[64,1024]{1,0:T(8,128)(2,1)S(1)}, u32[]{:S(2)}, u32[]{:S(2)}) collective-permute-start(bf16[64,1024]{1,0:T(8,128)(2,1)S(1)} %get-tuple-element.33), channel_id=1, source_target_pairs={{1,0},{2,1},{3,2},{4,3},{5,4},{6,5},{7,6},{8,7},{9,8},{10,9},{11,1... | collective-permute-start | bytes 393224 | tf_op jit(solution)/shard_map/ppermute | solution.py:17
  13.9 2.0 gather_fusion.7
  15.9 2.0 gather_fusion.6
  17.9 2.0 gather_fusion.5
  19.8 2.0 gather_fusion.4
  21.8 2.0 gather_fusion.3
  23.8 2.0 gather_fusion.2
  25.8 2.0 gather_fusion.1
  27.7 2.0 gather_fusion
  29.7 2.9 %fusion.77 = (f32[256]{0:T(256)S(1)}, f32[256,1024]{1,0:T(8,128)S(1)}) fusion(bf16[256,1024]{1,0:T(8,128)(2,1)} %gather_fusion.7, bf16[256,1024]{1,0:T(8,128)(2,1)} %gather_fusion.6, bf16[256,1024]{1,0:T(8,128)(2,1)} %gather_fusion.5, bf16[256,1024]{1,0:T(8,128)(2,1)} %gather_fusion.4, bf16[256,1024]{1,0:T(8,128)(2,1)} %gather_fusion.3, ...), kind=kLoop, calls=%fused_computation.151 | loop fusion | flops 4980480 | bytes 5768192 | tf_op jit(solution)/shard_map/reduce_sum | solution.py:29
  34.4 17.5 %collective-permute-start.8 = (f32[100,256]{1,0:T(8,128)S(1)}, f32[100,256]{1,0:T(8,128)S(1)}, u32[]{:S(2)}, u32[]{:S(2)}) collective-permute-start(f32[100,256]{1,0:T(8,128)S(1)} %convolution_bitcast_fusion), channel_id=1, source_target_pairs={{0,448},{64,0},{128,64},{192,128},{256,192},{320,256},{384,320},{4... | collective-permute-start | bytes 307208 | tf_op jit(solution)/shard_map/ppermute | solution.py:24
  51.9 1.9 collective-permute-start.5
  53.8 2.7 %collective-permute-start.4 = (f32[100,256]{1,0:T(8,128)S(1)}, f32[100,256]{1,0:T(8,128)S(1)}, u32[]{:S(2)}, u32[]{:S(2)}) collective-permute-start(f32[100,256]{1,0:T(8,128)S(1)} %convolution_bitcast_fusion), channel_id=1, source_target_pairs={{0,192},{64,256},{128,320},{192,384},{256,448},{320,0},{384,64},{4... | collective-permute-start | bytes 307208 | tf_op jit(solution)/shard_map/ppermute | solution.py:24
  56.5 11.7 %collective-permute-start.7 = (f32[100,256]{1,0:T(8,128)S(1)}, f32[100,256]{1,0:T(8,128)S(1)}, u32[]{:S(2)}, u32[]{:S(2)}) collective-permute-start(f32[100,256]{1,0:T(8,128)S(1)} %convolution_bitcast_fusion), channel_id=1, source_target_pairs={{0,384},{64,448},{128,0},{192,64},{256,128},{320,192},{384,256},{4... | collective-permute-start | bytes 307208 | tf_op jit(solution)/shard_map/ppermute | solution.py:24
  68.3 1.9 collective-permute-start.3
  70.2 5.6 %collective-permute-start.2 = (f32[100,256]{1,0:T(8,128)S(1)}, f32[100,256]{1,0:T(8,128)S(1)}, u32[]{:S(2)}, u32[]{:S(2)}) collective-permute-start(f32[100,256]{1,0:T(8,128)S(1)} %convolution_bitcast_fusion), channel_id=1, source_target_pairs={{0,64},{64,128},{128,192},{192,256},{256,320},{320,384},{384,448},... | collective-permute-start | bytes 307208 | tf_op jit(solution)/shard_map/ppermute | solution.py:24
  75.8 10.7 %collective-permute-start.6 = (f32[100,256]{1,0:T(8,128)S(1)}, f32[100,256]{1,0:T(8,128)S(1)}, u32[]{:S(2)}, u32[]{:S(2)}) collective-permute-start(f32[100,256]{1,0:T(8,128)S(1)} %convolution_bitcast_fusion), channel_id=1, source_target_pairs={{0,320},{64,384},{128,448},{192,0},{256,64},{320,128},{384,192},{4... | collective-permute-start | bytes 307208 | tf_op jit(solution)/shard_map/ppermute | solution.py:24
  86.6 2.6 collective-permute-done.2
  92.9 3.9 %scatter_custom_fusion = f32[384,1024]{1,0:T(8,128)} fusion(s32[256]{0:T(256)S(1)} %bitcast.75, f32[]{:T(128)} %constant.95.clone.1, f32[256,1024]{1,0:T(8,128)S(1)} %subtract_multiply_fusion, f32[]{:T(128)} %constant.94.clone.1), kind=kCustom, calls=%fused_computation.37 | custom fusion | flops 524288 | bytes 2621448 | tf_op jit(solution)/shard_map/scatter-add | solution.py:98
  96.8 5.2 %scatter_custom_fusion.1 = f32[384,1024]{1,0:T(8,128)} fusion(f32[384,1024]{1,0:T(8,128)} %scatter_custom_fusion, s32[256]{0:T(256)S(1)} %bitcast.73, f32[256,1024]{1,0:T(8,128)S(1)} %subtract_multiply_fusion, f32[]{:T(128)} %constant.94.clone.1), kind=kCustom, calls=%fused_computation.51 | custom fusion | flops 524288 | bytes 2621952 | tf_op jit(solution)/shard_map/scatter-add | solution.py:98
  102.0 5.2 %scatter_custom_fusion.2 = f32[384,1024]{1,0:T(8,128)} fusion(f32[384,1024]{1,0:T(8,128)} %scatter_custom_fusion.1, s32[256]{0:T(256)S(1)} %bitcast.71, f32[256,1024]{1,0:T(8,128)S(1)} %subtract_multiply_fusion, f32[]{:T(128)} %constant.94.clone.1), kind=kCustom, calls=%fused_computation.49 | custom fusion | flops 524288 | bytes 2621952 | tf_op jit(solution)/shard_map/scatter-add | solution.py:98
  107.2 5.2 %scatter_custom_fusion.3 = f32[384,1024]{1,0:T(8,128)} fusion(f32[384,1024]{1,0:T(8,128)} %scatter_custom_fusion.2, s32[256]{0:T(256)S(1)} %bitcast.69, f32[256,1024]{1,0:T(8,128)S(1)} %subtract_multiply_fusion, f32[]{:T(128)} %constant.94.clone.1), kind=kCustom, calls=%fused_computation.47 | custom fusion | flops 524288 | bytes 2621952 | tf_op jit(solution)/shard_map/scatter-add | solution.py:98
  112.4 5.2 %scatter_custom_fusion.4 = f32[384,1024]{1,0:T(8,128)} fusion(f32[384,1024]{1,0:T(8,128)} %scatter_custom_fusion.3, s32[256]{0:T(256)S(1)} %bitcast.67, f32[256,1024]{1,0:T(8,128)S(1)} %subtract_multiply_fusion, f32[]{:T(128)} %constant.94.clone.1), kind=kCustom, calls=%fused_computation.45 | custom fusion | flops 524288 | bytes 2621952 | tf_op jit(solution)/shard_map/scatter-add | solution.py:98
  117.6 5.2 %scatter_custom_fusion.5 = f32[384,1024]{1,0:T(8,128)} fusion(f32[384,1024]{1,0:T(8,128)} %scatter_custom_fusion.4, s32[256]{0:T(256)S(1)} %bitcast.65, f32[256,1024]{1,0:T(8,128)S(1)} %subtract_multiply_fusion, f32[]{:T(128)} %constant.94.clone.1), kind=kCustom, calls=%fused_computation.43 | custom fusion | flops 524288 | bytes 2621952 | tf_op jit(solution)/shard_map/scatter-add | solution.py:98
  122.8 5.2 %scatter_custom_fusion.6 = f32[384,1024]{1,0:T(8,128)} fusion(f32[384,1024]{1,0:T(8,128)} %scatter_custom_fusion.5, s32[256]{0:T(256)S(1)} %bitcast.63, f32[256,1024]{1,0:T(8,128)S(1)} %subtract_multiply_fusion, f32[]{:T(128)} %constant.94.clone.1), kind=kCustom, calls=%fused_computation.41 | custom fusion | flops 524288 | bytes 2621952 | tf_op jit(solution)/shard_map/scatter-add | solution.py:98
  128.0 5.2 %scatter_custom_fusion.7 = f32[384,1024]{1,0:T(8,128)} fusion(f32[384,1024]{1,0:T(8,128)} %scatter_custom_fusion.6, s32[256]{0:T(256)S(1)} %bitcast.61, f32[256,1024]{1,0:T(8,128)S(1)} %subtract_multiply_fusion, f32[]{:T(128)} %constant.94.clone.1), kind=kCustom, calls=%fused_computation.39 | custom fusion | flops 524288 | bytes 2621952 | tf_op jit(solution)/shard_map/scatter-add | solution.py:98
  134.9 9.4 %collective-permute-start.9 = (bf16[64,1024]{1,0:T(8,128)(2,1)S(1)}, bf16[64,1024]{1,0:T(8,128)(2,1)S(1)}, u32[]{:S(2)}, u32[]{:S(2)}) collective-permute-start(bf16[64,1024]{1,0:T(8,128)(2,1)S(1)} %get-tuple-element.30), channel_id=1, source_target_pairs={{0,1},{1,2},{2,3},{3,4},{4,5},{5,6},{6,7},{7,8},{8,9},{9,10},{10,1... | collective-permute-start | bytes 393224 | tf_op jit(solution)/shard_map/ppermute | solution.py:16
  144.3 1.9 collective-permute-start.10
  146.2 2.1 multiply_reduce_fusion.2
  149.7 108.2 %psum.7 = f32[]{:T(128)} all-reduce(f32[]{:T(128)} %multiply_reduce_fusion.2), channel_id=1, replica_groups=mesh['ens'=8,'grid'=64] {'ens','grid'}, use_global_device_ids=true, to_apply=%region_13.0 | all-reduce | flops 1 | bytes 8 | tf_op jit(solution)/shard_map/psum | solution.py:74
  262.0 2.1 convert_bitcast_fusion
  (74 shorter events, 15.0 us)
Async XLA Ops:
  0.6 32.2 %copy-start = (bf16[1024,1024]{1,0:T(8,128)(2,1)S(1)}, bf16[1024,1024]{1,0:T(8,128)(2,1)}, u32[]{:S(2)}) copy-start(bf16[1024,1024]{1,0:T(8,128)(2,1)} %param.13) | copy-start | bytes 6291460
  1.8 10.9 %collective-permute-start = (bf16[64,1024]{1,0:T(8,128)(2,1)S(1)}, bf16[64,1024]{1,0:T(8,128)(2,1)S(1)}, u32[]{:S(2)}, u32[]{:S(2)}) collective-permute-start(bf16[64,1024]{1,0:T(8,128)(2,1)S(1)} %get-tuple-element.32), channel_id=1, source_target_pairs={{0,1},{1,2},{2,3},{3,4},{4,5},{5,6},{6,7},{7,8},{8,9},{9,10},{10,1... | collective-permute-start | bytes 393224 | tf_op jit(solution)/shard_map/ppermute | solution.py:16
  6.4 6.5 %collective-permute-start.1 = (bf16[64,1024]{1,0:T(8,128)(2,1)S(1)}, bf16[64,1024]{1,0:T(8,128)(2,1)S(1)}, u32[]{:S(2)}, u32[]{:S(2)}) collective-permute-start(bf16[64,1024]{1,0:T(8,128)(2,1)S(1)} %get-tuple-element.33), channel_id=1, source_target_pairs={{1,0},{2,1},{3,2},{4,3},{5,4},{6,5},{7,6},{8,7},{9,8},{10,9},{11,1... | collective-permute-start | bytes 393224 | tf_op jit(solution)/shard_map/ppermute | solution.py:17
  27.7 2.0 copy-start.2
  29.7 3.2 %copy-start.16 = (f32[1024]{0:T(1024)S(1)}, f32[1024]{0:T(1024)}, u32[]{:S(2)}) copy-start(f32[1024]{0:T(1024)} %param.14) | copy-start | bytes 12292
  32.9 0.9 copy-start.18
  33.8 56.6 %copy-start.5 = (f32[100,256]{1,0:T(8,128)S(1)}, f32[100,256]{1,0:T(8,128)}, u32[]{:S(2)}) copy-start(f32[100,256]{1,0:T(8,128)} %param.16) | copy-start | bytes 307204
  33.8 56.6 %copy-start.17 = (f32[256]{0:T(256)S(1)}, f32[256]{0:T(256)}, u32[]{:S(2)}) copy-start(f32[256]{0:T(256)} %param.17) | copy-start | bytes 3076
  34.4 55.1 %copy-start.7 = (f32[100,256]{1,0:T(8,128)}, f32[100,256]{1,0:T(8,128)S(1)}, u32[]{:S(2)}) copy-start(f32[100,256]{1,0:T(8,128)S(1)} %convolution_bitcast_fusion) | copy-start | bytes 307204
  34.4 35.8 %collective-permute-start.8 = (f32[100,256]{1,0:T(8,128)S(1)}, f32[100,256]{1,0:T(8,128)S(1)}, u32[]{:S(2)}, u32[]{:S(2)}) collective-permute-start(f32[100,256]{1,0:T(8,128)S(1)} %convolution_bitcast_fusion), channel_id=1, source_target_pairs={{0,448},{64,0},{128,64},{192,128},{256,192},{320,256},{384,320},{4... | collective-permute-start | bytes 307208 | tf_op jit(solution)/shard_map/ppermute | solution.py:24
  51.9 23.9 %collective-permute-start.5 = (f32[100,256]{1,0:T(8,128)S(1)}, f32[100,256]{1,0:T(8,128)S(1)}, u32[]{:S(2)}, u32[]{:S(2)}) collective-permute-start(f32[100,256]{1,0:T(8,128)S(1)} %convolution_bitcast_fusion), channel_id=1, source_target_pairs={{0,256},{64,320},{128,384},{192,448},{256,0},{320,64},{384,128},{4... | collective-permute-start | bytes 307208 | tf_op jit(solution)/shard_map/ppermute | solution.py:24
  53.8 32.7 %collective-permute-start.4 = (f32[100,256]{1,0:T(8,128)S(1)}, f32[100,256]{1,0:T(8,128)S(1)}, u32[]{:S(2)}, u32[]{:S(2)}) collective-permute-start(f32[100,256]{1,0:T(8,128)S(1)} %convolution_bitcast_fusion), channel_id=1, source_target_pairs={{0,192},{64,256},{128,320},{192,384},{256,448},{320,0},{384,64},{4... | collective-permute-start | bytes 307208 | tf_op jit(solution)/shard_map/ppermute | solution.py:24
  56.5 30.0 %collective-permute-start.7 = (f32[100,256]{1,0:T(8,128)S(1)}, f32[100,256]{1,0:T(8,128)S(1)}, u32[]{:S(2)}, u32[]{:S(2)}) collective-permute-start(f32[100,256]{1,0:T(8,128)S(1)} %convolution_bitcast_fusion), channel_id=1, source_target_pairs={{0,384},{64,448},{128,0},{192,64},{256,128},{320,192},{384,256},{4... | collective-permute-start | bytes 307208 | tf_op jit(solution)/shard_map/ppermute | solution.py:24
  68.3 18.3 %collective-permute-start.3 = (f32[100,256]{1,0:T(8,128)S(1)}, f32[100,256]{1,0:T(8,128)S(1)}, u32[]{:S(2)}, u32[]{:S(2)}) collective-permute-start(f32[100,256]{1,0:T(8,128)S(1)} %convolution_bitcast_fusion), channel_id=1, source_target_pairs={{0,128},{64,192},{128,256},{192,320},{256,384},{320,448},{384,0},{... | collective-permute-start | bytes 307208 | tf_op jit(solution)/shard_map/ppermute | solution.py:24
  70.2 19.3 %copy-start.9 = (f32[100,256]{1,0:T(8,128)}, f32[100,256]{1,0:T(8,128)S(1)}, u32[]{:S(2)}) copy-start(f32[100,256]{1,0:T(8,128)S(1)} %collective-permute-done.8) | copy-start | bytes 307204
  70.2 18.9 %collective-permute-start.2 = (f32[100,256]{1,0:T(8,128)S(1)}, f32[100,256]{1,0:T(8,128)S(1)}, u32[]{:S(2)}, u32[]{:S(2)}) collective-permute-start(f32[100,256]{1,0:T(8,128)S(1)} %convolution_bitcast_fusion), channel_id=1, source_target_pairs={{0,64},{64,128},{128,192},{192,256},{256,320},{320,384},{384,448},... | collective-permute-start | bytes 307208 | tf_op jit(solution)/shard_map/ppermute | solution.py:24
  75.8 13.7 %copy-start.10 = (f32[100,256]{1,0:T(8,128)}, f32[100,256]{1,0:T(8,128)S(1)}, u32[]{:S(2)}) copy-start(f32[100,256]{1,0:T(8,128)S(1)} %collective-permute-done.5) | copy-start | bytes 307204
  75.8 13.7 %collective-permute-start.6 = (f32[100,256]{1,0:T(8,128)S(1)}, f32[100,256]{1,0:T(8,128)S(1)}, u32[]{:S(2)}, u32[]{:S(2)}) collective-permute-start(f32[100,256]{1,0:T(8,128)S(1)} %convolution_bitcast_fusion), channel_id=1, source_target_pairs={{0,320},{64,384},{128,448},{192,0},{256,64},{320,128},{384,192},{4... | collective-permute-start | bytes 307208 | tf_op jit(solution)/shard_map/ppermute | solution.py:24
  86.5 3.0 %copy-start.11 = (f32[100,256]{1,0:T(8,128)}, f32[100,256]{1,0:T(8,128)S(1)}, u32[]{:S(2)}) copy-start(f32[100,256]{1,0:T(8,128)S(1)} %collective-permute-done.4) | copy-start | bytes 307204
  86.6 3.0 %copy-start.12 = (f32[100,256]{1,0:T(8,128)}, f32[100,256]{1,0:T(8,128)S(1)}, u32[]{:S(2)}) copy-start(f32[100,256]{1,0:T(8,128)S(1)} %collective-permute-done.7) | copy-start | bytes 307204
  86.6 3.0 %copy-start.13 = (f32[100,256]{1,0:T(8,128)}, f32[100,256]{1,0:T(8,128)S(1)}, u32[]{:S(2)}) copy-start(f32[100,256]{1,0:T(8,128)S(1)} %collective-permute-done.3) | copy-start | bytes 307204
  89.1 0.7 copy-start.14
  89.8 0.6 copy-start.15
  91.1 1.4 copy-start.3
  133.2 13.0 %copy-start.6 = (f32[100,256]{1,0:T(8,128)S(1)}, f32[100,256]{1,0:T(8,128)}, u32[]{:S(2)}) copy-start(f32[100,256]{1,0:T(8,128)} %param.16) | copy-start | bytes 307204
  133.2 13.0 %copy-start.8 = (f32[100,256]{1,0:T(8,128)S(1)}, f32[100,256]{1,0:T(8,128)}, u32[]{:S(2)}) copy-start(f32[100,256]{1,0:T(8,128)} %copy-done.7) | copy-start | bytes 307204
  133.2 15.2 %copy-start.1 = (f32[384,1024]{1,0:T(8,128)S(1)}, f32[384,1024]{1,0:T(8,128)}, u32[]{:S(2)}) copy-start(f32[384,1024]{1,0:T(8,128)} %scatter_custom_fusion.7) | copy-start | bytes 4718596
  133.2 15.2 %copy-start.4 = (f32[256,1024]{1,0:T(8,128)S(1)}, f32[256,1024]{1,0:T(8,128)}, u32[]{:S(2)}) copy-start(f32[256,1024]{1,0:T(8,128)} %copy-done.3) | copy-start | bytes 3145732
  134.9 123.7 %collective-permute-start.9 = (bf16[64,1024]{1,0:T(8,128)(2,1)S(1)}, bf16[64,1024]{1,0:T(8,128)(2,1)S(1)}, u32[]{:S(2)}, u32[]{:S(2)}) collective-permute-start(bf16[64,1024]{1,0:T(8,128)(2,1)S(1)} %get-tuple-element.30), channel_id=1, source_target_pairs={{0,1},{1,2},{2,3},{3,4},{4,5},{5,6},{6,7},{7,8},{8,9},{9,10},{10,1... | collective-permute-start | bytes 393224 | tf_op jit(solution)/shard_map/ppermute | solution.py:16
  144.3 114.3 %collective-permute-start.10 = (bf16[64,1024]{1,0:T(8,128)(2,1)S(1)}, bf16[64,1024]{1,0:T(8,128)(2,1)}, u32[]{:S(2)}, u32[]{:S(2)}) collective-permute-start(bf16[64,1024]{1,0:T(8,128)(2,1)S(1)} %get-tuple-element.31), channel_id=1, source_target_pairs={{1,0},{2,1},{3,2},{4,3},{5,4},{6,5},{7,6},{8,7},{9,8},{10,9},{11,1... | collective-permute-start | bytes 393224 | tf_op jit(solution)/shard_map/ppermute | solution.py:17
where the time goes:
time: 266 us; the launch traced here: 265 us
  blocking collectives  108 us (41%)
  starting transfers between devices  73.4 us (28%)
  other arithmetic  56.2 us (21%)
  local copies, waits for them, and re-layouts  18 us (7%)
  matrix products  3.42 us (1%)
  waiting for transfers between devices  3.08 us (1%)
  between operations  2.86 us (1%)
    psum x1, blocking collectives, shards(): loss = lax.psum(local_loss, ('ens', 'grid')) / (total_points * vars_count)  108 us
    ppermute x7, starting transfers between devices, shifted(): lax.ppermute(shard, axis, [(i, (i + by) % size) for i in range(size)])  52 us
    scatter-add x8, other arithmetic, shards(): ext_grad = ext_grad.at[local_index[k]].add(spread_back)  40.3 us
    gather x8, local copies, waits for them, and re-layouts, shards(): summed = summed + extended[local_index[k]].astype(jnp.float32)  15.7 us
    ppermute x2, starting transfers between devices, extended_2(): before = lax.ppermute(last, axis, up)  14 us
    ppermute x2, starting transfers between devices, extended_2(): after = lax.ppermute(first, axis, down)  7.41 us
  transfers between devices with their start and end apart: 11, of which 3 were waited for; matrix products, arithmetic and copies ran while one was open for 2% of the time, Pallas kernels for 0%

commit v1 on v0

v1 whole, which is shorter than its diff:
```python
import functools

import jax
import jax.numpy as jnp
from jax import lax
from jax.experimental import pallas as pl
from jax.experimental.pallas import tpu as pltpu
from jax.sharding import PartitionSpec as P

ZH, XN, ZL, YN, CORES = 2, 4, 8, 4, 2
MESH = pl.DeviceIdType.MESH
GAP = 0.01
F32, BF16 = jnp.float32, jnp.bfloat16


def dot(a, b, ca, cb):
    return lax.dot_general(a, b, (((ca,), (cb,)), ((), ())), preferred_element_type=F32)


def device(zh, x, zl, y, core):
    return (zh * XN + x, (zl * YN + y) * CORES + core)


def kernel(
    total_points,
    x_hbm,
    nb_hbm,
    w_hbm,
    gain_hbm,
    proj_hbm,
    ver_hbm,
    area_hbm,
    out_ref,
    loss_ref,
    ext,
    w,
    pin,
    pv,
    nb,
    gain,
    ver,
    area,
    vert,
    areat,
    at_i,
    at_e,
    unit,
    scale,
    slope,
    fld,
    gs,
    direct,
    gmb,
    gsend,
    garr,
    lacc,
    lone,
    ltwo,
    in_sem,
    halo_s,
    halo_r,
    fld_s,
    fld_r,
    gh_s,
    gh_r,
    l1_s,
    l1_r,
    l2_s,
    l2_r,
):
    rows, c_dim = x_hbm.shape
    rim = rows // 4
    half = rows // 2
    vars_n = proj_hbm.shape[0]
    lanes = pv.shape[0]
    members = ZH * XN
    e, g = lax.axis_index("ens"), lax.axis_index("grid")
    bands = lax.axis_size("grid")
    zh, x = e // XN, e % XN
    zl, y, core = g // (YN * CORES), (g // CORES) % YN, g % CORES
    has_left, has_right = g > 0, g < bands - 1
    left, right = (e, g - 1), (e, g + 1)

    def at_z(d, core_):
        z = (zh * ZL + zl + d + 2 * ZH * ZL) % (ZH * ZL)
        return device(z // ZL, x, z % ZL, y, core_)

    offsets = [d for d in range(-(ZL // 2) + 1, ZL // 2 + 1) if d]
    xy = [(dx, dy) for dx in range(XN) for dy in range(YN) if (dx, dy) != (0, 0)]
    to_xy = [device(zh, (x + dx) % XN, zl, (y + dy) % YN, core) for dx, dy in xy]
    zc = [(d, dc) for d in offsets for dc in range(CORES)]
    to_zc = [at_z(d, (core + dc) % CORES) for d, dc in zc]
    from_zc = [at_z(-d, (core + dc) % CORES) for d, dc in zc]
    other_core = device(zh, x, zl, y, 1 - core)
    partner = device(1 - zh, x, zl, y, core)
    to_x = [device(zh, (x + dx) % XN, zl, y, core) for dx in range(1, XN)]

    barrier = pltpu.get_barrier_semaphore()

    def hello(to):
        pl.semaphore_signal(barrier, inc=1, device_id=to, device_id_type=MESH)

    hello(partner)
    for to in from_zc + to_xy:
        hello(to)
    pl.when(has_left)(lambda: hello(left))
    pl.when(has_right)(lambda: hello(right))

    loads = [
        pltpu.make_async_copy(nb_hbm, nb, in_sem.at[0]),
        pltpu.make_async_copy(x_hbm, ext.at[pl.ds(rim, rows)], in_sem.at[1]),
        pltpu.make_async_copy(gain_hbm, gain, in_sem.at[2]),
        pltpu.make_async_copy(w_hbm, w, in_sem.at[3]),
        pltpu.make_async_copy(proj_hbm, pin, in_sem.at[4]),
        pltpu.make_async_copy(ver_hbm, ver, in_sem.at[5]),
        pltpu.make_async_copy(area_hbm, area, in_sem.at[6]),
    ]
    for load in loads:
        load.start()

    @pl.when(jnp.logical_not(has_left))
    def _():
        ext[0:rim] = jnp.zeros((rim, c_dim), BF16)

    @pl.when(jnp.logical_not(has_right))
    def _():
        ext[rim + rows :] = jnp.zeros((rim, c_dim), BF16)

    loads[0].wait()
    near = pltpu.roll(nb[...] - (g * rows - rim), rows - rim, axis=1)

    def counts(first, size, lo):
        q = lax.broadcasted_iota(jnp.int32, (size, half), 0) + first
        total = jnp.zeros((size, half), F32)
        for k in range(nb.shape[0]):
            total = total + jnp.where(q == near[k : k + 1, lo : lo + half], 1.0, 0.0)
        return total.astype(BF16)

    at_i[...] = counts(rim, rows, 0)
    at_e[...] = counts(0, rows + 2 * rim, half)

    def forward(c, state, at, window):
        mixed = state.astype(F32) + dot(at, window, 0, 0) * (1.0 / nb.shape[0])
        centre = mixed - jnp.mean(mixed, axis=-1, keepdims=True)
        r = lax.rsqrt(jnp.mean(centre * centre, axis=-1, keepdims=True) + 1e-05)
        xh = centre * r
        here = pl.ds(c * half, half)
        unit[here] = xh
        scale[here] = jnp.broadcast_to(r, (half, scale.shape[1]))
        normed = (xh * gain[...]).astype(BF16)
        pre = dot(normed, w[...], 1, 0)
        k0 = 0.7978845608028654
        sq = pre * pre
        t = jnp.tanh(k0 * pre * (1.0 + 0.044715 * sq))
        cdf = 0.5 * (1.0 + t)
        out = (state.astype(F32) + pre * cdf).astype(BF16)
        slope[here] = cdf + 0.5 * pre * (1.0 - t * t) * (k0 * (1.0 + 3 * 0.044715 * sq))
        fld[c, e] = dot(out, pv[...], 1, 1).astype(BF16)

    loads[1].wait()
    loads[2].wait()
    loads[3].wait()
    loads[4].wait()
    pv[0 : vars_n // 16 * 16] = pin[0 : vars_n // 16 * 16]
    pv[vars_n // 16 * 16 :] = jnp.zeros((lanes - vars_n // 16 * 16, c_dim), BF16)
    pv[vars_n // 16 * 16 : vars_n] = pin[vars_n // 16 * 16 :]
    forward(0, ext[rim + rim : rim + rim + half], at_i[...], ext[rim : rim + rows])

    pl.semaphore_wait(
        barrier, 1 + len(to_zc) + len(to_xy) + has_left.astype(jnp.int32) + has_right.astype(jnp.int32)
    )

    def remote(src, dst, s_sem, r_sem, to):
        return pltpu.make_async_remote_copy(
            src_ref=src, dst_ref=dst, send_sem=s_sem, recv_sem=r_sem, device_id=to, device_id_type=MESH
        )

    halo_left = remote(
        ext.at[pl.ds(rim, rim)], ext.at[pl.ds(rim + rows, rim)], halo_s.at[0], halo_r.at[1], left
    )
    halo_right = remote(
        ext.at[pl.ds(rows, rim)], ext.at[pl.ds(0, rim)], halo_s.at[1], halo_r.at[0], right
    )
    from_left = remote(ext.at[pl.ds(0, rim)], ext.at[pl.ds(0, rim)], halo_s.at[0], halo_r.at[0], left)
    from_right = remote(
        ext.at[pl.ds(rim + rows, rim)],
        ext.at[pl.ds(rim + rows, rim)],
        halo_s.at[1],
        halo_r.at[1],
        right,
    )
    pl.when(has_left)(halo_left.start)
    pl.when(has_right)(halo_right.start)

    mate = (1 - zh) * XN + x

    def field(c, member, i, to):
        slot = fld.at[c, member]
        return remote(slot, slot, fld_s.at[c, i], fld_r.at[c, member], to)

    sent = []

    def send_own(c):
        for i, to in enumerate([partner] + to_x):
            copy = field(c, e, i, to)
            copy.start()
            sent.append(copy)

    def relay(c):
        field(c, mate, 0, partner).wait_recv()
        for i, to in enumerate(to_x):
            copy = field(c, mate, XN + i, to)
            copy.start()
            sent.append(copy)

    send_own(0)
    pl.when(has_left)(from_left.wait_recv)
    pl.when(has_right)(from_right.wait_recv)
    state_e = jnp.concatenate([ext[rows : rows + rim], ext[rim : 2 * rim]], axis=0)
    forward(1, state_e, at_e[...], ext[...])
    send_own(1)

    loads[5].wait()
    loads[6].wait()
    tall = jnp.concatenate([ver[...], jnp.zeros((lanes - vars_n, rows), F32)], axis=0)
    vert[...] = pltpu.roll(tall, rows - rim, axis=1).T
    areat[...] = pltpu.roll(jnp.broadcast_to(area[...], (lanes, rows)), rows - rim, axis=1).T
    lacc[...] = jnp.zeros(lacc.shape, F32)

    def score(c):
        step = 32

        def some(i, carry):
            at = pl.ds(pl.multiple_of(i * step, step), step)
            there = pl.ds(pl.multiple_of(c * half + i * step, step), step)
            f = [
                [fld[c, h * XN + (x + dx) % XN, at, :].astype(F32) for dx in range(XN)]
                for h in range(ZH)
            ]
            truth, weight = vert[there], areat[there]
            kept = {}
            for h in range(ZH):
                d = f[h][0] - truth
                q = d * d + GAP
                root = lax.rsqrt(q)
                good, pull = q * root, d * root
                spread = jnp.zeros_like(d)
                push = jnp.zeros_like(d)
                for dx in range(XN):
                    for h2 in range(ZH):
                        if (h2, dx) == (h, 0):
                            continue
                        if (h, h2, dx) == (1, 0, 0):
                            s, sp = kept["s"], -kept["sp"]
                        else:
                            d = f[h][0] - f[h2][dx]
                            q = d * d + GAP
                            root = lax.rsqrt(q)
                            s, sp = q * root, d * root
                        if (h, h2, dx) == (0, 1, 0):
                            kept["s"], kept["sp"] = s, sp
                        spread, push = spread + s, push + sp
                pair = 1.0 / (members * (members - 1))
                kept[h] = weight * (pull * (1.0 / members) - pair * push)
                part = weight * (good * (1.0 / members) - (0.5 * pair) * spread)
                lacc[...] += sum(part[8 * j : 8 * j + 8] for j in range(step // 8))
            gs[there] = jnp.where(zh == 0, kept[0], kept[1]).astype(BF16)
            return carry

        lax.fori_loop(0, half // step, some, 0)

    def backward(c):
        here = pl.ds(c * half, half)
        grad_y = dot(gs[here], pv[...], 1, 0)
        grad_pre = (grad_y * slope[here]).astype(BF16)
        gx = dot(grad_pre, w[...], 1, 1) * gain[...]
        xh = unit[here]
        flat = jnp.mean(gx, axis=-1, keepdims=True)
        lean = jnp.mean(gx * xh, axis=-1, keepdims=True)
        gm = scale[here][:, 0:1] * (gx - flat - xh * lean)
        direct[here] = grad_y + gm
        gmb[here] = gm.astype(BF16)

    def others(c):
        for dx in range(1, XN):
            field(c, zh * XN + (x + dx) % XN, 0, partner).wait_recv()
            field(c, (1 - zh) * XN + (x + dx) % XN, 0, partner).wait_recv()

    relay(0)
    others(0)
    score(0)
    backward(0)
    relay(1)
    others(1)
    score(1)

    lane = lax.broadcasted_iota(jnp.int32, (1, lanes), 1)
    mine1 = x * YN + y
    lone[mine1] = jnp.where(lane < vars_n, jnp.sum(lacc[...], axis=0, keepdims=True), 0.0)
    for i, to in enumerate(to_xy):
        copy = remote(lone.at[mine1], lone.at[mine1], l1_s.at[i], l1_r.at[mine1], to)
        copy.start()
        sent.append(copy)

    backward(1)
    per = 1.0 / nb.shape[0]
    gsend[0] = (dot(at_e[0:rim], gmb[half:], 1, 0) * per).astype(BF16)
    gsend[1] = (dot(at_e[rim + rows :], gmb[half:], 1, 0) * per).astype(BF16)
    grad_left = remote(gsend.at[0], garr.at[1], gh_s.at[0], gh_r.at[1], left)
    grad_right = remote(gsend.at[1], garr.at[0], gh_s.at[1], gh_r.at[0], right)
    pl.when(has_left)(grad_left.start)
    pl.when(has_right)(grad_right.start)

    for dx, dy in xy:
        slot = ((x + dx) % XN) * YN + (y + dy) % YN
        remote(lone.at[slot], lone.at[slot], l1_s.at[0], l1_r.at[slot], other_core).wait_recv()
    mine2 = zl * CORES + core
    acc = lone[0]
    for i in range(1, XN * YN):
        acc = acc + lone[i]
    ltwo[mine2] = acc
    for i, to in enumerate([other_core] + to_zc):
        copy = remote(ltwo.at[mine2], ltwo.at[mine2], l2_s.at[i], l2_r.at[mine2], to)
        copy.start()
        sent.append(copy)

    spread = (dot(at_i[...], gmb[0:half], 1, 0) + dot(at_e[rim : rim + rows], gmb[half:], 1, 0)) * per
    out_ref[rim : rim + half] = (spread[rim : rim + half] + direct[0:half]).astype(BF16)
    tail = spread[rows - rim :] + direct[half : half + rim]
    head = spread[0:rim] + direct[half + rim :]
    direct[half : half + rim] = tail
    direct[half + rim :] = head

    @pl.when(jnp.logical_not(has_left))
    def _():
        garr[0] = jnp.zeros((rim, c_dim), BF16)

    @pl.when(jnp.logical_not(has_right))
    def _():
        garr[1] = jnp.zeros((rim, c_dim), BF16)

    @pl.when(has_left)
    def _():
        remote(garr.at[0], garr.at[0], gh_s.at[0], gh_r.at[0], left).wait_recv()

    @pl.when(has_right)
    def _():
        remote(garr.at[1], garr.at[1], gh_s.at[1], gh_r.at[1], right).wait_recv()

    out_ref[0:rim] = (direct[half + rim :] + garr[0].astype(F32)).astype(BF16)
    out_ref[rows - rim :] = (direct[half : half + rim] + garr[1].astype(F32)).astype(BF16)

    for slot in range(ZL * CORES):

        @pl.when(slot != mine2)
        def _():
            remote(ltwo.at[slot], ltwo.at[slot], l2_s.at[0], l2_r.at[slot], other_core).wait_recv()

    acc = ltwo[0]
    for i in range(1, ZL * CORES):
        acc = acc + ltwo[i]
    loss_ref[0, 0] = jnp.sum(acc) * (1.0 / (total_points * vars_n))

    for copy in sent:
        copy.wait_send()
    pl.when(has_left)(halo_left.wait_send)
    pl.when(has_right)(halo_right.wait_send)
    pl.when(has_left)(grad_left.wait_send)
    pl.when(has_right)(grad_right.wait_send)


def shards(
    latent_fields, neighbours, mix_weight, norm_gain, output_projector, verifying_fields, area
):
    _, rows, c_dim = latent_fields.shape
    count = neighbours.shape[0]
    vars_n = output_projector.shape[0]
    rim, half, lanes = rows // 4, rows // 2, 128
    members = ZH * XN
    anywhere = pl.BlockSpec(memory_space=pl.ANY)
    dma = pltpu.SemaphoreType.DMA
    n_xy, n_zc = XN * YN, ZL * CORES
    out, loss = pl.pallas_call(
        functools.partial(kernel, rows * lax.axis_size("grid")),
        out_shape=(
            jax.ShapeDtypeStruct((rows, c_dim), BF16),
            jax.ShapeDtypeStruct((1, 1), F32),
        ),
        in_specs=[anywhere] * 7,
        out_specs=(
            pl.BlockSpec(memory_space=pltpu.VMEM),
            pl.BlockSpec(memory_space=pltpu.SMEM),
        ),
        scratch_shapes=[
            pltpu.VMEM((rows + 2 * rim, c_dim), BF16),
            pltpu.VMEM(mix_weight.shape, BF16),
            pltpu.VMEM((vars_n, c_dim), BF16),
            pltpu.VMEM((lanes, c_dim), BF16),
            pltpu.VMEM((count, rows), jnp.int32),
            pltpu.VMEM((1, c_dim), F32),
            pltpu.VMEM((vars_n, rows), F32),
            pltpu.VMEM((1, rows), F32),
            pltpu.VMEM((rows, lanes), F32),
            pltpu.VMEM((rows, lanes), F32),
            pltpu.VMEM((rows, half), BF16),
            pltpu.VMEM((rows + 2 * rim, half), BF16),
            pltpu.VMEM((rows, c_dim), F32),
            pltpu.VMEM((rows, lanes), F32),
            pltpu.VMEM((rows, c_dim), F32),
            pltpu.VMEM((2, members, half, lanes), BF16),
            pltpu.VMEM((rows, lanes), BF16),
            pltpu.VMEM((rows, c_dim), F32),
            pltpu.VMEM((rows, c_dim), BF16),
            pltpu.VMEM((2, rim, c_dim), BF16),
            pltpu.VMEM((2, rim, c_dim), BF16),
            pltpu.VMEM((8, lanes), F32),
            pltpu.VMEM((n_xy, 1, lanes), F32),
            pltpu.VMEM((n_zc, 1, lanes), F32),
            dma((7,)),
            dma((2,)),
            dma((2,)),
            dma((2, 2 * XN)),
            dma((2, members)),
            dma((2,)),
            dma((2,)),
            dma((n_xy,)),
            dma((n_xy,)),
            dma((n_zc,)),
            dma((n_zc,)),
        ],
        compiler_params=pltpu.CompilerParams(
            collective_id=0, has_side_effects=True, vmem_limit_bytes=63 << 20
        ),
        name="crps_layer",
    )(
        latent_fields.reshape(rows, c_dim),
        neighbours,
        mix_weight,
        norm_gain.reshape(1, c_dim),
        output_projector,
        verifying_fields,
        area.reshape(1, rows),
    )
    return (out[None], loss.reshape(()))


def solution(mesh):
    in_specs = (P("ens", "grid", None), P(None, "grid"), P(), P(), P(), P(None, "grid"), P("grid"))
    out_specs = (P("ens", "grid", None), P())
    return jax.shard_map(shards, mesh=mesh, in_specs=in_specs, out_specs=out_specs, check_vma=False)
```

time: 266 us -> 50.5 us (0.19)
  blocking collectives: 108 us -> 0 us
  starting transfers between devices: 73.4 us -> 0 us
  other arithmetic: 56.2 us -> 0 us
  Pallas kernels: 0 us -> 46.1 us
  local copies, waits for them, and re-layouts: 18 us -> 1.87 us
  matrix products: 3.42 us -> 0 us
  waiting for transfers between devices: 3.08 us -> 0 us
    psum x1 -> x0, blocking collectives: 108 us -> none  [shards(): loss = lax.psum(local_loss, ('ens', 'grid')) / (total_points * vars_count)]
    ppermute x11 -> x0, starting transfers between devices: 73.4 us -> none  [the longest x7 52 us: shifted(): lax.ppermute(shard, axis, [(i, (i + by) % size) for i in range(size)])]
    pallas_call x0 -> x1, Pallas kernels: none -> 46.1 us  [shards(): pl.pallas_call(functools.partial(kernel, rows * lax.axis_size('grid')), o...]
    scatter-add x10 -> x0, other arithmetic: 43.7 us -> none  [the longest x8 40.3 us: shards(): ext_grad = ext_grad.at[local_index[k]].add(spread_back)]
    gather x8 -> x0, local copies, waits for them, and re-layouts: 15.7 us -> none  [shards(): summed = summed + extended[local_index[k]].astype(jnp.float32)]
    reduce_sum x3 -> x0, other arithmetic: 5.24 us -> none  [the longest x1 2.88 us: layer_forward(): centre = mixed - jnp.mean(mixed, axis=-1, keepdims=True)]
    dot_general x4 -> x0, matrix products: 3.42 us -> none  [the longest x1 1.42 us: shards(): lax.dot_general(grad_pre, mix_weight, (((1,), (1,)), ((), ())), preferred...]
    ppermute x11 -> x0, waiting for transfers between devices: 3.08 us -> none  [the longest x7 2.96 us: shifted(): lax.ppermute(shard, axis, [(i, (i + by) % size) for i in range(size)])]
  transfers between devices with their start and end apart: 11 -> 0, of which waited for: 3 -> 0; matrix products, arithmetic and copies ran while one was open for 2% -> 0% of each run, Pallas kernels for 0% -> 0%
where the time goes in v1:
time: 50.5 us; the launch traced here: 50.3 us
  Pallas kernels  46.1 us (91%)
  between operations  2.34 us (5%)
  local copies, waits for them, and re-layouts  1.87 us (4%)
    pallas_call x1, Pallas kernels, shards(): pl.pallas_call(functools.partial(kernel, rows * lax.axis_size('grid')), o...  46.1 us
    unnamed x1, local copies, waits for them, and re-layouts  1.87 us

profile of v1, /device:TPU:1, one launch (start us, length us, event | category | flops | bytes accessed | tf_op | source)
XLA Modules:
  0.0 50.3 jit_solution(14984090775365348486)
XLA Ops:
  0.6 46.1 %crps_layer.1 = (bf16[256,1024]{1,0:T(8,128)(2,1)}, f32[1,1]{1,0:T(1,128)}) custom-call(bf16[256,1024]{1,0:T(8,128)(2,1)} %bitcast.6, s32[8,256]{1,0:T(8,128)} %nb_hbm.1, bf16[1024,1024]{1,0:T(8,128)(2,1)} %w_hbm.1, f32[1,1024]{1,0:T(1,128)} %bitcast.7, bf16[100,1024]{1,0:T(8,128)(2,1)} %proj_hbm.1, f32[100,256]{1,0:T(8,128)} %ver_hbm.1, f32[1,256]{1,0:T(1,128)} %bitcast.8), custom_call_target="tpu_custom_call" | custom-call | tf_op jit(solution)/shard_map/crps_layer/pallas_call | solution.py:383
  46.7 1.9 %copy.11 = bf16[1,256,1024]{2,1,0:T(8,128)(2,1)} copy(bf16[1,256,1024]{2,1,0:T(8,128)(2,1)} %bitcast.5) | data formatting | bytes 1048576

commit v2 on v1

--- a/solution.py
+++ b/solution.py
@@ -48,6 +48,8 @@
     scale,
     slope,
     fld,
+    fq,
+    gq,
     gs,
     direct,
     gmb,
@@ -56,11 +58,15 @@
     lacc,
     lone,
     ltwo,
+    near_sem,
+    far_sem,
     in_sem,
     halo_s,
     halo_r,
     fld_s,
     fld_r,
+    g_s,
+    g_r,
     gh_s,
     gh_r,
     l1_s,
@@ -74,6 +80,7 @@
     vars_n = proj_hbm.shape[0]
     lanes = pv.shape[0]
     members = ZH * XN
+    part = half // XN
     e, g = lax.axis_index("ens"), lax.axis_index("grid")
     bands = lax.axis_size("grid")
     zh, x = e // XN, e % XN
@@ -90,21 +97,35 @@
     to_xy = [device(zh, (x + dx) % XN, zl, (y + dy) % YN, core) for dx, dy in xy]
     zc = [(d, dc) for d in offsets for dc in range(CORES)]
     to_zc = [at_z(d, (core + dc) % CORES) for d, dc in zc]
-    from_zc = [at_z(-d, (core + dc) % CORES) for d, dc in zc]
     other_core = device(zh, x, zl, y, 1 - core)
-    partner = device(1 - zh, x, zl, y, core)
-    to_x = [device(zh, (x + dx) % XN, zl, y, core) for dx in range(1, XN)]
+    meet = [(dh, dx) for dx in range(XN) for dh in range(ZH) if (dh, dx) != (0, 0)]
+    to_meet = [device((zh + dh) % ZH, (x + dx) % XN, zl, y, core) for dh, dx in meet]
 
     barrier = pltpu.get_barrier_semaphore()
 
     def hello(to):
         pl.semaphore_signal(barrier, inc=1, device_id=to, device_id_type=MESH)
 
-    hello(partner)
-    for to in from_zc + to_xy:
+    chip, chips = g // CORES, bands // CORES
+    first, last = chip == 0, chip == chips - 1
+    upper = core == 1
+    far_hellos = (
+        [device(zh, (x + dx) % XN, zl, (y + dy) % YN, 1) for dx, dy in xy]
+        + [device(1 - zh, (x + dx) % XN, zl, y, 1) for dx in range(XN)]
+        + [at_z(-d, 1) for d in offsets]
+    )
+
+    @pl.when(upper)
+    def _():
+        hello((e, g - 1))
+        pl.when(jnp.logical_not(last))(lambda: hello((e, g + 1)))
+
+    @pl.when(jnp.logical_and(jnp.logical_not(upper), jnp.logical_not(first)))
+    def _():
+        hello((e, g - CORES))
+
+    for to in far_hellos:
         hello(to)
-    pl.when(has_left)(lambda: hello(left))
-    pl.when(has_right)(lambda: hello(right))
 
     loads = [
         pltpu.make_async_copy(nb_hbm, nb, in_sem.at[0]),
@@ -126,6 +147,46 @@
     def _():
         ext[rim + rows :] = jnp.zeros((rim, c_dim), BF16)
 
+    def near_wait():
+        @pl.when(jnp.logical_not(upper))
+        def _():
+            pl.semaphore_wait(barrier, 3 - first.astype(jnp.int32) - last.astype(jnp.int32))
+            pl.semaphore_signal(near_sem, inc=1, device_id=other_core, device_id_type=MESH)
+
+        @pl.when(upper)
+        def _():
+            pl.semaphore_wait(near_sem, 1)
+
+    def far_wait():
+        @pl.when(upper)
+        def _():
+            pl.semaphore_wait(barrier, CORES * len(far_hellos))
+            pl.semaphore_signal(far_sem, inc=1, device_id=other_core, device_id_type=MESH)
+
+        @pl.when(jnp.logical_not(upper))
+        def _():
+            pl.semaphore_wait(far_sem, 1)
+
+    def remote(src, dst, s_sem, r_sem, to):
+        return pltpu.make_async_remote_copy(
+            src_ref=src, dst_ref=dst, send_sem=s_sem, recv_sem=r_sem, device_id=to, device_id_type=MESH
+        )
+
+    halo_left = remote(
+        x_hbm.at[pl.ds(0, rim)], ext.at[pl.ds(rim + rows, rim)], halo_s.at[0], halo_r.at[1], left
+    )
+    halo_right = remote(
+        x_hbm.at[pl.ds(rows - rim, rim)], ext.at[pl.ds(0, rim)], halo_s.at[1], halo_r.at[0], right
+    )
+    from_left = remote(ext.at[pl.ds(0, rim)], ext.at[pl.ds(0, rim)], halo_s.at[0], halo_r.at[0], left)
+    from_right = remote(
+        ext.at[pl.ds(rim + rows, rim)],
+        ext.at[pl.ds(rim + rows, rim)],
+        halo_s.at[1],
+        halo_r.at[1],
+        right,
+    )
+
     loads[0].wait()
     near = pltpu.roll(nb[...] - (g * rows - rim), rows - rim, axis=1)
 
@@ -138,6 +199,9 @@
 
     at_i[...] = counts(rim, rows, 0)
     at_e[...] = counts(0, rows + 2 * rim, half)
+    near_wait()
+    pl.when(has_left)(halo_left.start)
+    pl.when(has_right)(halo_right.start)
 
     def forward(c, state, at, window):
         mixed = state.astype(F32) + dot(at, window, 0, 0) * (1.0 / nb.shape[0])
@@ -155,7 +219,8 @@
         cdf = 0.5 * (1.0 + t)
         out = (state.astype(F32) + pre * cdf).astype(BF16)
         slope[here] = cdf + 0.5 * pre * (1.0 - t * t) * (k0 * (1.0 + 3 * 0.044715 * sq))
-        fld[c, e] = dot(out, pv[...], 1, 1).astype(BF16)
+        fld[c] = dot(out, pv[...], 1, 1).astype(BF16)
+        fq[c, e] = fld[c, pl.ds(pl.multiple_of(x * part, part), part)]
 
     loads[1].wait()
     loads[2].wait()
@@ -166,59 +231,33 @@
     pv[vars_n // 16 * 16 : vars_n] = pin[vars_n // 16 * 16 :]
     forward(0, ext[rim + rim : rim + rim + half], at_i[...], ext[rim : rim + rows])
 
-    pl.semaphore_wait(
-        barrier, 1 + len(to_zc) + len(to_xy) + has_left.astype(jnp.int32) + has_right.astype(jnp.int32)
-    )
-
-    def remote(src, dst, s_sem, r_sem, to):
-        return pltpu.make_async_remote_copy(
-            src_ref=src, dst_ref=dst, send_sem=s_sem, recv_sem=r_sem, device_id=to, device_id_type=MESH
-        )
-
-    halo_left = remote(
-        ext.at[pl.ds(rim, rim)], ext.at[pl.ds(rim + rows, rim)], halo_s.at[0], halo_r.at[1], left
-    )
-    halo_right = remote(
-        ext.at[pl.ds(rows, rim)], ext.at[pl.ds(0, rim)], halo_s.at[1], halo_r.at[0], right
-    )
-    from_left = remote(ext.at[pl.ds(0, rim)], ext.at[pl.ds(0, rim)], halo_s.at[0], halo_r.at[0], left)
-    from_right = remote(
-        ext.at[pl.ds(rim + rows, rim)],
-        ext.at[pl.ds(rim + rows, rim)],
-        halo_s.at[1],
-        halo_r.at[1],
-        right,
-    )
-    pl.when(has_left)(halo_left.start)
-    pl.when(has_right)(halo_right.start)
-
-    mate = (1 - zh) * XN + x
-
-    def field(c, member, i, to):
-        slot = fld.at[c, member]
-        return remote(slot, slot, fld_s.at[c, i], fld_r.at[c, member], to)
-
     sent = []
 
-    def send_own(c):
-        for i, to in enumerate([partner] + to_x):
-            copy = field(c, e, i, to)
-            copy.start()
-            sent.append(copy)
-
-    def relay(c):
-        field(c, mate, 0, partner).wait_recv()
-        for i, to in enumerate(to_x):
-            copy = field(c, mate, XN + i, to)
-            copy.start()
-            sent.append(copy)
-
-    send_own(0)
+    def field(c, i):
+        (dh, dx), to = meet[i], to_meet[i]
+        there = pl.ds(pl.multiple_of(((x + dx) % XN) * part, part), part)
+        return remote(fld.at[c, there], fq.at[c, e], fld_s.at[c, i], fld_r.at[c, e], to)
+
+    def send_fields(c):
+        for i in range(len(meet)):
+            field(c, i).start()
+
+    @pl.when(zh > 0)
+    def _():
+        far_wait()
+        send_fields(0)
+
     pl.when(has_left)(from_left.wait_recv)
     pl.when(has_right)(from_right.wait_recv)
     state_e = jnp.concatenate([ext[rows : rows + rim], ext[rim : 2 * rim]], axis=0)
     forward(1, state_e, at_e[...], ext[...])
-    send_own(1)
+
+    @pl.when(zh == 0)
+    def _():
+        far_wait()
+        send_fields(0)
+
+    send_fields(1)
 
     loads[5].wait()
     loads[6].wait()
@@ -228,46 +267,54 @@
     lacc[...] = jnp.zeros(lacc.shape, F32)
 
     def score(c):
-        step = 32
-
-        def some(i, carry):
-            at = pl.ds(pl.multiple_of(i * step, step), step)
-            there = pl.ds(pl.multiple_of(c * half + i * step, step), step)
-            f = [
-                [fld[c, h * XN + (x + dx) % XN, at, :].astype(F32) for dx in range(XN)]
-                for h in range(ZH)
-            ]
+        for dh, dx in meet:
+            m = ((zh + dh) % ZH) * XN + (x + dx) % XN
+            remote(fq.at[c, m], fq.at[c, m], fld_s.at[c, 0], fld_r.at[c, m], other_core).wait_recv()
+        pair = 1.0 / (members * (members - 1))
+        step = 16
+        for lo in range(0, part, step):
+            f = [fq[c, m, lo : lo + step, :].astype(F32) for m in range(members)]
+            there = pl.ds(pl.multiple_of(c * half + x * part + lo, step), step)
             truth, weight = vert[there], areat[there]
-            kept = {}
-            for h in range(ZH):
-                d = f[h][0] - truth
+            good = jnp.zeros_like(truth)
+            spread = jnp.zeros_like(truth)
+            pull = []
+            for m in range(members):
+                d = f[m] - truth
                 q = d * d + GAP
                 root = lax.rsqrt(q)
-                good, pull = q * root, d * root
-                spread = jnp.zeros_like(d)
-                push = jnp.zeros_like(d)
-                for dx in range(XN):
-                    for h2 in range(ZH):
-                        if (h2, dx) == (h, 0):
-                            continue
-                        if (h, h2, dx) == (1, 0, 0):
-                            s, sp = kept["s"], -kept["sp"]
-                        else:
-                            d = f[h][0] - f[h2][dx]
-                            q = d * d + GAP
-                            root = lax.rsqrt(q)
-                            s, sp = q * root, d * root
-                        if (h, h2, dx) == (0, 1, 0):
-                            kept["s"], kept["sp"] = s, sp
-                        spread, push = spread + s, push + sp
-                pair = 1.0 / (members * (members - 1))
-                kept[h] = weight * (pull * (1.0 / members) - pair * push)
-                part = weight * (good * (1.0 / members) - (0.5 * pair) * spread)
-                lacc[...] += sum(part[8 * j : 8 * j + 8] for j in range(step // 8))
-            gs[there] = jnp.where(zh == 0, kept[0], kept[1]).astype(BF16)
-            return carry
-
-        lax.fori_loop(0, half // step, some, 0)
+                good = good + q * root
+                pull.append((1.0 / members) * (d * root))
+            for m in range(members):
+                for n in range(m + 1, members):
+                    d = f[m] - f[n]
+                    q = d * d + GAP
+                    root = lax.rsqrt(q)
+                    spread = spread + q * root
+                    slant = pair * (d * root)
+                    pull[m] = pull[m] - slant
+                    pull[n] = pull[n] + slant
+            total = weight * (good * (1.0 / members) - pair * spread)
+            lacc[...] += total[0:8] + total[8:16]
+            for i in range(XN):
+                mine = jnp.where(zh == 0, pull[i], pull[XN + i])
+                gq[c, i, lo : lo + step, :] = (weight * mine).astype(BF16)
+
+    def give(c, dx):
+        to = device(zh, (x + dx) % XN, zl, y, core)
+        here = gs.at[pl.ds(pl.multiple_of(c * half + x * part, part), part)]
+        return remote(gq.at[c, (x + dx) % XN], here, g_s.at[c, dx], g_r.at[c, x], to)
+
+    def send_g(c):
+        for dx in range(1, XN):
+            give(c, dx).start()
+        gs[pl.ds(pl.multiple_of(c * half + x * part, part), part)] = gq[c, x]
+
+    def wait_g(c):
+        for dx in range(1, XN):
+            i = (x + dx) % XN
+            here = gs.at[pl.ds(pl.multiple_of(c * half + i * part, part), part)]
+            remote(here, here, g_s.at[c, 0], g_r.at[c, i], other_core).wait_recv()
 
     def backward(c):
         here = pl.ds(c * half, half)
@@ -281,17 +328,8 @@
         direct[here] = grad_y + gm
         gmb[here] = gm.astype(BF16)
 
-    def others(c):
-        for dx in range(1, XN):
-            field(c, zh * XN + (x + dx) % XN, 0, partner).wait_recv()
-            field(c, (1 - zh) * XN + (x + dx) % XN, 0, partner).wait_recv()
-
-    relay(0)
-    others(0)
     score(0)
-    backward(0)
-    relay(1)
-    others(1)
+    send_g(0)
     score(1)
 
     lane = lax.broadcasted_iota(jnp.int32, (1, lanes), 1)
@@ -302,6 +340,10 @@
         copy.start()
         sent.append(copy)
 
+    send_g(1)
+    wait_g(0)
+    backward(0)
+    wait_g(1)
     backward(1)
     per = 1.0 / nb.shape[0]
     gsend[0] = (dot(at_e[0:rim], gmb[half:], 1, 0) * per).astype(BF16)
@@ -359,14 +401,27 @@
     acc = ltwo[0]
     for i in range(1, ZL * CORES):
         acc = acc + ltwo[i]
-    loss_ref[0, 0] = jnp.sum(acc) * (1.0 / (total_points * vars_n))
+    loss = jnp.sum(acc, axis=-1, keepdims=True) * (1.0 / (total_points * vars_n))
+    loss_ref[...] = jnp.broadcast_to(loss, loss_ref.shape)
 
     for copy in sent:
         copy.wait_send()
+    for c in range(2):
+        for i in range(len(meet)):
+            field(c, i).wait_send()
+        for dx in range(1, XN):
+            give(c, dx).wait_send()
     pl.when(has_left)(halo_left.wait_send)
     pl.when(has_right)(halo_right.wait_send)
     pl.when(has_left)(grad_left.wait_send)
     pl.when(has_right)(grad_right.wait_send)
+
+
+def store(made, total, out_hbm, loss_ref, sem):
+    copy = pltpu.make_async_copy(made, out_hbm, sem)
+    copy.start()
+    loss_ref[...] = total[:, 0:1]
+    copy.wait()
 
 
 def shards(
@@ -383,13 +438,13 @@
     out, loss = pl.pallas_call(
         functools.partial(kernel, rows * lax.axis_size("grid")),
         out_shape=(
-            jax.ShapeDtypeStruct((rows, c_dim), BF16),
-            jax.ShapeDtypeStruct((1, 1), F32),
+            pltpu.VMEM((rows, c_dim), BF16),
+            pltpu.VMEM((1, lanes), F32),
         ),
         in_specs=[anywhere] * 7,
         out_specs=(
             pl.BlockSpec(memory_space=pltpu.VMEM),
-            pl.BlockSpec(memory_space=pltpu.SMEM),
+            pl.BlockSpec(memory_space=pltpu.VMEM),
         ),
         scratch_shapes=[
             pltpu.VMEM((rows + 2 * rim, c_dim), BF16),
@@ -407,7 +462,9 @@
             pltpu.VMEM((rows, c_dim), F32),
             pltpu.VMEM((rows, lanes), F32),
             pltpu.VMEM((rows, c_dim), F32),
-            pltpu.VMEM((2, members, half, lanes), BF16),
+            pltpu.VMEM((2, half, lanes), BF16),
+            pltpu.VMEM((2, members, half // XN, lanes), BF16),
+            pltpu.VMEM((2, XN, half // XN, lanes), BF16),
             pltpu.VMEM((rows, lanes), BF16),
             pltpu.VMEM((rows, c_dim), F32),
             pltpu.VMEM((rows, c_dim), BF16),
@@ -416,11 +473,15 @@
             pltpu.VMEM((8, lanes), F32),
             pltpu.VMEM((n_xy, 1, lanes), F32),
             pltpu.VMEM((n_zc, 1, lanes), F32),
+            pltpu.SemaphoreType.REGULAR,
+            pltpu.SemaphoreType.REGULAR,
             dma((7,)),
             dma((2,)),
             dma((2,)),
-            dma((2, 2 * XN)),
             dma((2, members)),
+            dma((2, members)),
+            dma((2, XN)),
+            dma((2, XN)),
             dma((2,)),
             dma((2,)),
             dma((n_xy,)),
@@ -441,6 +502,18 @@
         verifying_fields,
         area.reshape(1, rows),
     )
+    out, loss = pl.pallas_call(
+        store,
+        out_shape=(
+            jax.ShapeDtypeStruct((rows, c_dim), BF16),
+            jax.ShapeDtypeStruct((1, 1), F32),
+        ),
+        in_specs=[pl.BlockSpec(memory_space=pltpu.VMEM)] * 2,
+        out_specs=(anywhere, pl.BlockSpec(memory_space=pltpu.VMEM)),
+        scratch_shapes=[dma(())],
+        compiler_params=pltpu.CompilerParams(vmem_limit_bytes=16 << 20),
+        name="store_result",
+    )(out, loss)
     return (out[None], loss.reshape(()))
 
 

time: 50.5 us -> 43.5 us (0.86)
  Pallas kernels: 46.1 us -> 42.7 us
  local copies, waits for them, and re-layouts: 1.87 us -> 0 us
  between operations: 2.34 us -> 0.64 us
    pallas_call x1, Pallas kernels: 46.1 us -> 41.4 us  [shards(): pl.pallas_call(functools.partial(kernel, rows * lax.axis_size('grid')), o...]
    unnamed x1 -> x0, local copies, waits for them, and re-layouts: 1.87 us -> none
    pallas_call x0 -> x1, Pallas kernels: none -> 1.31 us  [shards(): pl.pallas_call(store, out_shape=(jax.ShapeDtypeStruct((rows, c_dim), BF16...]
where the time goes in v2:
time: 43.5 us; the launch traced here: 43.3 us
  Pallas kernels  42.7 us (98%)
  between operations  0.64 us (1%)
    pallas_call x1, Pallas kernels, shards(): pl.pallas_call(functools.partial(kernel, rows * lax.axis_size('grid')), o...  41.4 us
    pallas_call x1, Pallas kernels, shards(): pl.pallas_call(store, out_shape=(jax.ShapeDtypeStruct((rows, c_dim), BF16...  1.31 us

profile of v2, /device:TPU:1, one launch (start us, length us, event | category | flops | bytes accessed | tf_op | source)
XLA Modules:
  0.0 43.3 jit_solution(17545367505585890183)
XLA Ops:
  0.6 41.4 %crps_layer.1 = (bf16[256,1024]{1,0:T(8,128)(2,1)S(1)}, f32[1,128]{1,0:T(1,128)S(1)}) custom-call(bf16[256,1024]{1,0:T(8,128)(2,1)} %bitcast.5, s32[8,256]{1,0:T(8,128)} %nb_hbm.1, bf16[1024,1024]{1,0:T(8,128)(2,1)} %w_hbm.1, f32[1,1024]{1,0:T(1,128)} %bitcast.6, bf16[100,1024]{1,0:T(8,128)(2,1)} %proj_hbm.1, f32[100,256]{1,0:T(8,128)} %ver_hbm.1, ...), custom_call_target="tpu_custom_call" | custom-call | tf_op jit(solution)/shard_map/crps_layer/pallas_call | solution.py:438
  42.0 1.3 %store_result.1 = (bf16[256,1024]{1,0:T(8,128)(2,1)}, f32[1,1]{1,0:T(1,128)}) custom-call(bf16[256,1024]{1,0:T(8,128)(2,1)S(1)} %get-tuple-element.6.made, f32[1,128]{1,0:T(1,128)S(1)} %get-tuple-element.7.total), custom_call_target="tpu_custom_call" | custom-call | tf_op jit(solution)/shard_map/store_result/pallas_call | solution.py:505

commit v3 on v2

--- a/solution.py
+++ b/solution.py
@@ -124,9 +124,6 @@
     def _():
         hello((e, g - CORES))
 
-    for to in far_hellos:
-        hello(to)
-
     loads = [
         pltpu.make_async_copy(nb_hbm, nb, in_sem.at[0]),
         pltpu.make_async_copy(x_hbm, ext.at[pl.ds(rim, rows)], in_sem.at[1]),
@@ -138,6 +135,9 @@
     ]
     for load in loads:
         load.start()
+
+    for to in far_hellos:
+        hello(to)
 
     @pl.when(jnp.logical_not(has_left))
     def _():
@@ -231,12 +231,14 @@
     pv[vars_n // 16 * 16 : vars_n] = pin[vars_n // 16 * 16 :]
     forward(0, ext[rim + rim : rim + rim + half], at_i[...], ext[rim : rim + rows])
 
-    sent = []
-
     def field(c, i):
         (dh, dx), to = meet[i], to_meet[i]
         there = pl.ds(pl.multiple_of(((x + dx) % XN) * part, part), part)
-        return remote(fld.at[c, there], fq.at[c, e], fld_s.at[c, i], fld_r.at[c, e], to)
+        return remote(fld.at[c, there], fq.at[c, e], fld_s.at[c], fld_r.at[c], to)
+
+    def all_of(ref, count, s_sem, r_sem):
+        some = ref.at[pl.ds(0, count)]
+        return remote(some, some, s_sem, r_sem, other_core)
 
     def send_fields(c):
         for i in range(len(meet)):
@@ -267,9 +269,7 @@
     lacc[...] = jnp.zeros(lacc.shape, F32)
 
     def score(c):
-        for dh, dx in meet:
-            m = ((zh + dh) % ZH) * XN + (x + dx) % XN
-            remote(fq.at[c, m], fq.at[c, m], fld_s.at[c, 0], fld_r.at[c, m], other_core).wait_recv()
+        all_of(fq.at[c], len(meet), fld_s.at[c], fld_r.at[c]).wait_recv()
         pair = 1.0 / (members * (members - 1))
         step = 16
         for lo in range(0, part, step):
@@ -303,7 +303,7 @@
     def give(c, dx):
         to = device(zh, (x + dx) % XN, zl, y, core)
         here = gs.at[pl.ds(pl.multiple_of(c * half + x * part, part), part)]
-        return remote(gq.at[c, (x + dx) % XN], here, g_s.at[c, dx], g_r.at[c, x], to)
+        return remote(gq.at[c, (x + dx) % XN], here, g_s.at[c], g_r.at[c], to)
 
     def send_g(c):
         for dx in range(1, XN):
@@ -311,10 +311,7 @@
         gs[pl.ds(pl.multiple_of(c * half + x * part, part), part)] = gq[c, x]
 
     def wait_g(c):
-        for dx in range(1, XN):
-            i = (x + dx) % XN
-            here = gs.at[pl.ds(pl.multiple_of(c * half + i * part, part), part)]
-            remote(here, here, g_s.at[c, 0], g_r.at[c, i], other_core).wait_recv()
+        all_of(gq.at[c], XN - 1, g_s.at[c], g_r.at[c]).wait_recv()
 
     def backward(c):
         here = pl.ds(c * half, half)
@@ -335,10 +332,9 @@
     lane = lax.broadcasted_iota(jnp.int32, (1, lanes), 1)
     mine1 = x * YN + y
     lone[mine1] = jnp.where(lane < vars_n, jnp.sum(lacc[...], axis=0, keepdims=True), 0.0)
-    for i, to in enumerate(to_xy):
-        copy = remote(lone.at[mine1], lone.at[mine1], l1_s.at[i], l1_r.at[mine1], to)
+    for to in to_xy:
+        copy = remote(lone.at[mine1], lone.at[mine1], l1_s, l1_r, to)
         copy.start()
-        sent.append(copy)
 
     send_g(1)
     wait_g(0)
@@ -353,18 +349,16 @@
     pl.when(has_left)(grad_left.start)
     pl.when(has_right)(grad_right.start)
 
-    for dx, dy in xy:
-        slot = ((x + dx) % XN) * YN + (y + dy) % YN
-        remote(lone.at[slot], lone.at[slot], l1_s.at[0], l1_r.at[slot], other_core).wait_recv()
+    loss_one = all_of(lone, len(to_xy), l1_s, l1_r)
+    loss_one.wait_recv()
     mine2 = zl * CORES + core
     acc = lone[0]
     for i in range(1, XN * YN):
         acc = acc + lone[i]
     ltwo[mine2] = acc
-    for i, to in enumerate([other_core] + to_zc):
-        copy = remote(ltwo.at[mine2], ltwo.at[mine2], l2_s.at[i], l2_r.at[mine2], to)
+    for to in [other_core] + to_zc:
+        copy = remote(ltwo.at[mine2], ltwo.at[mine2], l2_s, l2_r, to)
         copy.start()
-        sent.append(copy)
 
     spread = (dot(at_i[...], gmb[0:half], 1, 0) + dot(at_e[rim : rim + rows], gmb[half:], 1, 0)) * per
     out_ref[rim : rim + half] = (spread[rim : rim + half] + direct[0:half]).astype(BF16)
@@ -392,25 +386,19 @@
     out_ref[0:rim] = (direct[half + rim :] + garr[0].astype(F32)).astype(BF16)
     out_ref[rows - rim :] = (direct[half : half + rim] + garr[1].astype(F32)).astype(BF16)
 
-    for slot in range(ZL * CORES):
-
-        @pl.when(slot != mine2)
-        def _():
-            remote(ltwo.at[slot], ltwo.at[slot], l2_s.at[0], l2_r.at[slot], other_core).wait_recv()
-
+    loss_two = all_of(ltwo, 1 + len(to_zc), l2_s, l2_r)
+    loss_two.wait_recv()
     acc = ltwo[0]
     for i in range(1, ZL * CORES):
         acc = acc + ltwo[i]
     loss = jnp.sum(acc, axis=-1, keepdims=True) * (1.0 / (total_points * vars_n))
     loss_ref[...] = jnp.broadcast_to(loss, loss_ref.shape)
 
-    for copy in sent:
-        copy.wait_send()
+    loss_one.wait_send()
+    loss_two.wait_send()
     for c in range(2):
-        for i in range(len(meet)):
-            field(c, i).wait_send()
-        for dx in range(1, XN):
-            give(c, dx).wait_send()
+        all_of(fq.at[c], len(meet), fld_s.at[c], fld_r.at[c]).wait_send()
+        all_of(gq.at[c], XN - 1, g_s.at[c], g_r.at[c]).wait_send()
     pl.when(has_left)(halo_left.wait_send)
     pl.when(has_right)(halo_right.wait_send)
     pl.when(has_left)(grad_left.wait_send)
@@ -478,16 +466,16 @@
             dma((7,)),
             dma((2,)),
             dma((2,)),
-            dma((2, members)),
-            dma((2, members)),
-            dma((2, XN)),
-            dma((2, XN)),
-            dma((2,)),
-            dma((2,)),
-            dma((n_xy,)),
-            dma((n_xy,)),
-            dma((n_zc,)),
-            dma((n_zc,)),
+            dma((2,)),
+            dma((2,)),
+            dma((2,)),
+            dma((2,)),
+            dma((2,)),
+            dma((2,)),
+            dma(()),
+            dma(()),
+            dma(()),
+            dma(()),
         ],
         compiler_params=pltpu.CompilerParams(
             collective_id=0, has_side_effects=True, vmem_limit_bytes=63 << 20

time: 43.5 us -> 42.3 us (0.972)
  Pallas kernels: 42.7 us -> 41.5 us
    pallas_call x1, Pallas kernels: 41.4 us -> 40.2 us  [shards(): pl.pallas_call(functools.partial(kernel, rows * lax.axis_size('grid')), o...]
where the time goes in v3:
time: 42.3 us; the launch traced here: 42.1 us
  Pallas kernels  41.5 us (98%)
  between operations  0.64 us (2%)
    pallas_call x1, Pallas kernels, shards(): pl.pallas_call(functools.partial(kernel, rows * lax.axis_size('grid')), o...  40.2 us
    pallas_call x1, Pallas kernels, shards(): pl.pallas_call(store, out_shape=(jax.ShapeDtypeStruct((rows, c_dim), BF16...  1.31 us

profile of v3, /device:TPU:1, one launch (start us, length us, event | category | flops | bytes accessed | tf_op | source)
XLA Modules:
  0.0 42.1 jit_solution(2729465747902959126)
XLA Ops:
  0.6 40.2 %crps_layer.1 = (bf16[256,1024]{1,0:T(8,128)(2,1)S(1)}, f32[1,128]{1,0:T(1,128)S(1)}) custom-call(bf16[256,1024]{1,0:T(8,128)(2,1)} %bitcast.5, s32[8,256]{1,0:T(8,128)} %nb_hbm.1, bf16[1024,1024]{1,0:T(8,128)(2,1)} %w_hbm.1, f32[1,1024]{1,0:T(1,128)} %bitcast.6, bf16[100,1024]{1,0:T(8,128)(2,1)} %proj_hbm.1, f32[100,256]{1,0:T(8,128)} %ver_hbm.1, ...), custom_call_target="tpu_custom_call" | custom-call | tf_op jit(solution)/shard_map/crps_layer/pallas_call | solution.py:426
  40.8 1.3 %store_result.1 = (bf16[256,1024]{1,0:T(8,128)(2,1)}, f32[1,1]{1,0:T(1,128)}) custom-call(bf16[256,1024]{1,0:T(8,128)(2,1)S(1)} %get-tuple-element.6.made, f32[1,128]{1,0:T(1,128)S(1)} %get-tuple-element.7.total), custom_call_target="tpu_custom_call" | custom-call | tf_op jit(solution)/shard_map/store_result/pallas_call | solution.py:493

commit v4 on v3

v4 whole, which is shorter than its diff:
```python
import functools

import jax
import jax.numpy as jnp
from jax import lax
from jax.experimental import pallas as pl
from jax.experimental.pallas import tpu as pltpu
from jax.sharding import PartitionSpec as P

ZH, XN, ZL, YN, CORES = 2, 4, 8, 4, 2
MESH = pl.DeviceIdType.MESH
GAP = 0.01
F32, BF16 = jnp.float32, jnp.bfloat16


def dot(a, b, ca, cb):
    return lax.dot_general(a, b, (((ca,), (cb,)), ((), ())), preferred_element_type=F32)


def device(zh, x, zl, y, core):
    return (zh * XN + x, (zl * YN + y) * CORES + core)


def kernel(
    total_points,
    x_hbm,
    nb_hbm,
    w_hbm,
    gain_hbm,
    proj_hbm,
    ver_hbm,
    area_hbm,
    out_ref,
    loss_ref,
    ext,
    w,
    pin,
    pv,
    nb,
    gain,
    ver,
    area,
    vert,
    tall,
    at0,
    at1,
    unit,
    scale,
    slope,
    fld,
    fq0,
    fq1,
    gq0,
    gq1,
    gs,
    direct,
    gmb,
    tot,
    gsend,
    garr,
    lacc,
    lone,
    ltwo,
    near_sem,
    far_sem,
    in_sem,
    halo_s,
    halo_r,
    fq_s,
    fq_r,
    gq_s,
    gq_r,
    gh_s,
    gh_r,
    l1_s,
    l1_r,
    l2_s,
    l2_r,
):
    rows, c_dim = x_hbm.shape
    rim = rows // 4
    half = rows // 2
    vars_n = proj_hbm.shape[0]
    lanes = pv.shape[0]
    members = ZH * XN
    e, g = lax.axis_index("ens"), lax.axis_index("grid")
    bands = lax.axis_size("grid")
    zh, x = e // XN, e % XN
    zl, y, core = g // (YN * CORES), (g // CORES) % YN, g % CORES
    chip, chips = g // CORES, bands // CORES
    first, last = chip == 0, chip == chips - 1
    upper = core == 1
    has_far = jnp.where(upper, jnp.logical_not(last), jnp.logical_not(first))
    far = (e, g - 1 + 2 * core)

    base, size = (0, rows - rim), (rows - rim, rim)
    share = tuple(n // XN for n in size)
    fq, gq = (fq0, fq1), (gq0, gq1)

    def at_multiple(start, n):
        return pl.ds(pl.multiple_of(start, 16), n)

    near_rows = at_multiple((1 - core) * (rows - rim), rim)
    far_rows = at_multiple(core * (rows - rim), rim)
    near_halo = at_multiple((1 - core) * (rows + rim), rim)
    far_halo = at_multiple(core * (rows + rim), rim)

    def at_z(d, core_):
        z = (zh * ZL + zl + d + ZH * ZL) % (ZH * ZL)
        return device(z // ZL, x, z % ZL, y, core_)

    offsets = [d for d in range(-(ZL // 2) + 1, ZL // 2 + 1) if d]
    xy = [(dx, dy) for dx in range(XN) for dy in range(YN) if (dx, dy) != (0, 0)]
    to_xy = [device(zh, (x + dx) % XN, zl, (y + dy) % YN, core) for dx, dy in xy]
    zc = [(d, dc) for d in offsets for dc in range(CORES)]
    to_zc = [at_z(d, (core + dc) % CORES) for d, dc in zc]
    other_core = device(zh, x, zl, y, 1 - core)
    to_x = [device(zh, (x + dx) % XN, zl, y, core) for dx in range(1, XN)]
    meet = [(dh, dx) for dh in range(ZH - 1, -1, -1) for dx in range(XN) if (dh, dx) != (0, 0)]
    to_meet = [device((zh + dh) % ZH, (x + dx) % XN, zl, y, core) for dh, dx in meet]

    barrier = pltpu.get_barrier_semaphore()

    def hello(to):
        pl.semaphore_signal(barrier, inc=1, device_id=to, device_id_type=MESH)

    far_hellos = (
        [device(1 - zh, (x + dx) % XN, zl, y, 1) for dx in range(XN)]
        + [at_z(-d, 1) for d in offsets]
        + [device(zh, (x + dx) % XN, zl, (y + dy) % YN, 1) for dx, dy in xy]
    )

    @pl.when(upper)
    def _():
        hello((e, g - 1))
        pl.when(jnp.logical_not(last))(lambda: hello((e, g + 1)))

    @pl.when(jnp.logical_and(jnp.logical_not(upper), jnp.logical_not(first)))
    def _():
        hello((e, g - CORES))

    loads = [
        pltpu.make_async_copy(nb_hbm, nb, in_sem.at[0]),
        pltpu.make_async_copy(x_hbm, ext.at[pl.ds(rim, rows)], in_sem.at[1]),
        pltpu.make_async_copy(gain_hbm, gain, in_sem.at[2]),
        pltpu.make_async_copy(w_hbm, w, in_sem.at[3]),
        pltpu.make_async_copy(proj_hbm, pin, in_sem.at[4]),
        pltpu.make_async_copy(ver_hbm, ver, in_sem.at[5]),
        pltpu.make_async_copy(area_hbm, area, in_sem.at[6]),
    ]
    for load in loads:
        load.start()

    for to in far_hellos:
        hello(to)

    @pl.when(jnp.logical_not(has_far))
    def _():
        ext[far_halo] = jnp.zeros((rim, c_dim), BF16)

    def near_wait():
        @pl.when(jnp.logical_not(upper))
        def _():
            pl.semaphore_wait(barrier, 3 - first.astype(jnp.int32) - last.astype(jnp.int32))
            pl.semaphore_signal(near_sem, inc=1, device_id=other_core, device_id_type=MESH)

        @pl.when(upper)
        def _():
            pl.semaphore_wait(near_sem, 1)

    def far_wait():
        @pl.when(upper)
        def _():
            pl.semaphore_wait(barrier, CORES * len(far_hellos))
            pl.semaphore_signal(far_sem, inc=1, device_id=other_core, device_id_type=MESH)

        @pl.when(jnp.logical_not(upper))
        def _():
            pl.semaphore_wait(far_sem, 1)

    def remote(src, dst, s_sem, r_sem, to):
        return pltpu.make_async_remote_copy(
            src_ref=src, dst_ref=dst, send_sem=s_sem, recv_sem=r_sem, device_id=to, device_id_type=MESH
        )

    halo_near = remote(
        x_hbm.at[near_rows],
        ext.at[at_multiple(core * (rows + rim), rim)],
        halo_s.at[0],
        halo_r.at[0],
        other_core,
    )
    halo_far = remote(
        x_hbm.at[far_rows],
        ext.at[at_multiple((1 - core) * (rows + rim), rim)],
        halo_s.at[1],
        halo_r.at[1],
        far,
    )
    from_near = remote(ext.at[near_halo], ext.at[near_halo], halo_s.at[0], halo_r.at[0], other_core)
    from_far = remote(ext.at[far_halo], ext.at[far_halo], halo_s.at[1], halo_r.at[1], far)

    loads[0].wait()
    near = pltpu.roll(nb[...] - (g * rows - rim), rows - rim, axis=1)
    ends = near[:, half:]
    near = jnp.concatenate([near[:, :half], jnp.where(upper, pltpu.roll(ends, rim, axis=1), ends)], axis=1)
    start0 = (1 - core) * rim
    start1 = core * (rows - rim)

    def counts(start, height, lo, width):
        q = lax.broadcasted_iota(jnp.int32, (height, width), 0) + start
        total = jnp.zeros((height, width), F32)
        for k in range(nb.shape[0]):
            total = total + jnp.where(q == near[k : k + 1, lo : lo + width], 1.0, 0.0)
        return total.astype(BF16)

    at0[...] = counts(start0, rows + rim, 0, size[0])
    at1[...] = counts(start1, rows - rim, base[1], size[1])
    near_wait()
    halo_near.start()
    pl.when(has_far)(halo_far.start)

    def forward(c, state, at, window):
        mixed = state.astype(F32) + dot(at, window, 0, 0) * (1.0 / nb.shape[0])
        centre = mixed - jnp.mean(mixed, axis=-1, keepdims=True)
        r = lax.rsqrt(jnp.mean(centre * centre, axis=-1, keepdims=True) + 1e-05)
        xh = centre * r
        here = pl.ds(base[c], size[c])
        unit[here] = xh
        scale[here] = jnp.broadcast_to(r, (size[c], scale.shape[1]))
        normed = (xh * gain[...]).astype(BF16)
        pre = dot(normed, w[...], 1, 0)
        k0 = 0.7978845608028654
        sq = pre * pre
        t = jnp.tanh(k0 * pre * (1.0 + 0.044715 * sq))
        cdf = 0.5 * (1.0 + t)
        out = (state.astype(F32) + pre * cdf).astype(BF16)
        slope[here] = cdf + 0.5 * pre * (1.0 - t * t) * (k0 * (1.0 + 3 * 0.044715 * sq))
        fld[here] = dot(out, pv[...], 1, 1).astype(BF16)
        fq[c][e] = fld[at_multiple(base[c] + x * share[c], share[c])]

    loads[1].wait()
    loads[2].wait()
    loads[3].wait()
    loads[4].wait()
    pv[0 : vars_n // 16 * 16] = pin[0 : vars_n // 16 * 16]
    pv[vars_n // 16 * 16 :] = jnp.zeros((lanes - vars_n // 16 * 16, c_dim), BF16)
    pv[vars_n // 16 * 16 : vars_n] = pin[vars_n // 16 * 16 :]
    from_near.wait_recv()
    quarter = ext[at_multiple(rim + (1 - core) * (rows - rim), rim)]
    state = jnp.concatenate([ext[2 * rim : 2 * rim + half], quarter], axis=0)
    forward(0, state, at0[...], ext[at_multiple(start0, rows + rim)])

    loads[5].wait()
    loads[6].wait()
    vert[0:vars_n] = ver[...]
    vert[vars_n:] = jnp.broadcast_to(area[...], (lanes - vars_n, rows))
    turned = pltpu.roll(vert[...], rows - rim, axis=1).T
    tall[0:half] = turned[0:half]
    tall[at_multiple(half + core * rim, rim)] = turned[half : half + rim]
    tall[at_multiple(half + (1 - core) * rim, rim)] = turned[half + rim :]
    lacc[...] = jnp.zeros(lacc.shape, F32)

    def shared(c, i):
        (dh, dx), to = meet[i], to_meet[i]
        there = at_multiple(base[c] + ((x + dx) % XN) * share[c], share[c])
        return remote(fld.at[there], fq[c].at[e], fq_s.at[c], fq_r.at[c], to)

    def send_fields(c):
        for i in range(len(meet)):
            shared(c, i).start()

    def all_of(ref, count, s_sem, r_sem):
        some = ref.at[pl.ds(0, count)]
        return remote(some, some, s_sem, r_sem, other_core)

    @pl.when(zh > 0)
    def _():
        far_wait()
        send_fields(0)

    pl.when(has_far)(from_far.wait_recv)
    quarter = ext[at_multiple(rim + core * (rows - rim), rim)]
    forward(1, quarter, at1[...], ext[at_multiple(start1, rows - rim)])

    @pl.when(zh == 0)
    def _():
        far_wait()
        send_fields(0)

    send_fields(1)

    lane = lax.broadcasted_iota(jnp.int32, (1, lanes), 1)
    pair = 1.0 / (members * (members - 1))

    def score(c):
        all_of(fq[c], len(meet), fq_s.at[c], fq_r.at[c]).wait_recv()
        step = 16
        for lo in range(0, share[c], step):
            f = [fq[c][m, lo : lo + step, :].astype(F32) for m in range(members)]
            want = tall[at_multiple(base[c] + x * share[c] + lo, step)]
            weight = want[:, lanes - 1 :]
            want = jnp.where(lane < vars_n, want, 0.0)
            good = jnp.zeros_like(want)
            spread = jnp.zeros_like(want)
            pull = []
            for m in range(members):
                d = f[m] - want
                q = d * d + GAP
                root = lax.rsqrt(q)
                good = good + q * root
                pull.append((1.0 / members) * (d * root))
            for m in range(members):
                for n in range(m + 1, members):
                    d = f[m] - f[n]
                    q = d * d + GAP
                    root = lax.rsqrt(q)
                    spread = spread + q * root
                    slant = pair * (d * root)
                    pull[m] = pull[m] - slant
                    pull[n] = pull[n] + slant
            total = weight * (good * (1.0 / members) - pair * spread)
            lacc[...] += total[0:8] + total[8:16]
            for i in range(XN):
                mine = jnp.where(zh == 0, pull[i], pull[XN + i])
                gq[c][i, lo : lo + step, :] = (weight * mine).astype(BF16)

    def send_g(c):
        here = at_multiple(base[c] + x * share[c], share[c])
        for dx in range(1, XN):
            src = gq[c].at[(x + dx) % XN]
            remote(src, gs.at[here], gq_s.at[c], gq_r.at[c], to_x[dx - 1]).start()
        gs[here] = gq[c][x]

    def wait_g(c):
        all_of(gq[c], XN - 1, gq_s.at[c], gq_r.at[c]).wait_recv()

    def backward(c):
        here = pl.ds(base[c], size[c])
        grad_y = dot(gs[here], pv[...], 1, 0)
        grad_pre = (grad_y * slope[here]).astype(BF16)
        gx = dot(grad_pre, w[...], 1, 1) * gain[...]
        xh = unit[here]
        flat = jnp.mean(gx, axis=-1, keepdims=True)
        lean = jnp.mean(gx * xh, axis=-1, keepdims=True)
        gm = scale[here][:, 0:1] * (gx - flat - xh * lean)
        direct[here] = grad_y + gm
        gmb[here] = gm.astype(BF16)

    score(0)
    send_g(0)
    score(1)
    mine1 = x * YN + y
    lone[mine1] = jnp.where(lane < vars_n, jnp.sum(lacc[...], axis=0, keepdims=True), 0.0)
    for to in to_xy:
        remote(lone.at[mine1], lone.at[mine1], l1_s, l1_r, to).start()
    send_g(1)
    per = 1.0 / nb.shape[0]

    wait_g(1)
    backward(1)
    block = gmb[base[1] :]
    gsend[1] = (dot(at1[at_multiple(core * half, rim), :], block, 1, 0) * per).astype(BF16)
    grad_far = remote(gsend.at[1], garr.at[1], gh_s.at[1], gh_r.at[1], far)
    pl.when(has_far)(grad_far.start)

    wait_g(0)
    backward(0)
    wide = gmb[0 : size[0]]
    gsend[0] = (dot(at0[at_multiple((1 - core) * rows, rim), :], wide, 1, 0) * per).astype(BF16)
    grad_near = remote(gsend.at[0], garr.at[0], gh_s.at[0], gh_r.at[0], other_core)
    grad_near.start()

    loss_one = all_of(lone, len(to_xy), l1_s, l1_r)
    loss_one.wait_recv()
    mine2 = zl * CORES + core
    acc = lone[0]
    for i in range(1, XN * YN):
        acc = acc + lone[i]
    ltwo[mine2] = acc
    for to in [other_core] + to_zc:
        remote(ltwo.at[mine2], ltwo.at[mine2], l2_s, l2_r, to).start()

    tot[...] = dot(at0[at_multiple(core * rim, rows), :], wide, 1, 0) * per
    tot[rim : rim + half] += direct[0:half]
    tot[near_rows] += direct[half : half + rim]
    tot[at_multiple(core * half, half)] += dot(at1[at_multiple((1 - core) * rim, half), :], block, 1, 0) * per
    tot[far_rows] += direct[base[1] :]
    remote(garr.at[0], garr.at[0], gh_s.at[0], gh_r.at[0], other_core).wait_recv()
    tot[near_rows] += garr[0].astype(F32)
    out_ref[...] = tot[...].astype(BF16)

    @pl.when(has_far)
    def _():
        remote(garr.at[1], garr.at[1], gh_s.at[1], gh_r.at[1], far).wait_recv()
        out_ref[far_rows] = (tot[far_rows] + garr[1].astype(F32)).astype(BF16)

    loss_two = all_of(ltwo, 1 + len(to_zc), l2_s, l2_r)
    loss_two.wait_recv()
    acc = ltwo[0]
    for i in range(1, ZL * CORES):
        acc = acc + ltwo[i]
    loss = jnp.sum(acc, axis=-1, keepdims=True) * (1.0 / (total_points * vars_n))
    loss_ref[...] = jnp.broadcast_to(loss, loss_ref.shape)

    loss_one.wait_send()
    loss_two.wait_send()
    for c in range(2):
        all_of(fq[c], len(meet), fq_s.at[c], fq_r.at[c]).wait_send()
        all_of(gq[c], XN - 1, gq_s.at[c], gq_r.at[c]).wait_send()
    halo_near.wait_send()
    grad_near.wait_send()
    pl.when(has_far)(halo_far.wait_send)
    pl.when(has_far)(grad_far.wait_send)


def store(made, total, out_hbm, loss_hbm, one, sem):
    copy = pltpu.make_async_copy(made, out_hbm, sem.at[0])
    copy.start()
    one[...] = total[:, 0:1]
    small = pltpu.make_async_copy(one, loss_hbm, sem.at[1])
    small.start()
    copy.wait()
    small.wait()


def shards(
    latent_fields, neighbours, mix_weight, norm_gain, output_projector, verifying_fields, area
):
    _, rows, c_dim = latent_fields.shape
    count = neighbours.shape[0]
    vars_n = output_projector.shape[0]
    rim, lanes = rows // 4, 128
    members = ZH * XN
    anywhere = pl.BlockSpec(memory_space=pl.ANY)
    dma = pltpu.SemaphoreType.DMA
    n_xy, n_zc = XN * YN, ZL * CORES
    out, loss = pl.pallas_call(
        functools.partial(kernel, rows * lax.axis_size("grid")),
        out_shape=(
            pltpu.VMEM((rows, c_dim), BF16),
            pltpu.VMEM((1, lanes), F32),
        ),
        in_specs=[anywhere] * 7,
        out_specs=(
            pl.BlockSpec(memory_space=pltpu.VMEM),
            pl.BlockSpec(memory_space=pltpu.VMEM),
        ),
        scratch_shapes=[
            pltpu.VMEM((rows + 2 * rim, c_dim), BF16),
            pltpu.VMEM(mix_weight.shape, BF16),
            pltpu.VMEM((vars_n, c_dim), BF16),
            pltpu.VMEM((lanes, c_dim), BF16),
            pltpu.VMEM((count, rows), jnp.int32),
            pltpu.VMEM((1, c_dim), F32),
            pltpu.VMEM((vars_n, rows), F32),
            pltpu.VMEM((1, rows), F32),
            pltpu.VMEM((lanes, rows), F32),
            pltpu.VMEM((rows, lanes), F32),
            pltpu.VMEM((rows + rim, rows - rim), BF16),
            pltpu.VMEM((rows - rim, rim), BF16),
            pltpu.VMEM((rows, c_dim), F32),
            pltpu.VMEM((rows, lanes), F32),
            pltpu.VMEM((rows, c_dim), F32),
            pltpu.VMEM((rows, lanes), BF16),
            pltpu.VMEM((members, (rows - rim) // XN, lanes), BF16),
            pltpu.VMEM((members, rim // XN, lanes), BF16),
            pltpu.VMEM((XN, (rows - rim) // XN, lanes), BF16),
            pltpu.VMEM((XN, rim // XN, lanes), BF16),
            pltpu.VMEM((rows, lanes), BF16),
            pltpu.VMEM((rows, c_dim), F32),
            pltpu.VMEM((rows, c_dim), BF16),
            pltpu.VMEM((rows, c_dim), F32),
            pltpu.VMEM((2, rim, c_dim), BF16),
            pltpu.VMEM((2, rim, c_dim), BF16),
            pltpu.VMEM((8, lanes), F32),
            pltpu.VMEM((n_xy, 1, lanes), F32),
            pltpu.VMEM((n_zc, 1, lanes), F32),
            pltpu.SemaphoreType.REGULAR,
            pltpu.SemaphoreType.REGULAR,
            dma((7,)),
            dma((2,)),
            dma((2,)),
            dma((2,)),
            dma((2,)),
            dma((2,)),
            dma((2,)),
            dma((2,)),
            dma((2,)),
            dma(()),
            dma(()),
            dma(()),
            dma(()),
        ],
        compiler_params=pltpu.CompilerParams(
            collective_id=0, has_side_effects=True, vmem_limit_bytes=63 << 20
        ),
        name="crps_layer",
    )(
        latent_fields.reshape(rows, c_dim),
        neighbours,
        mix_weight,
        norm_gain.reshape(1, c_dim),
        output_projector,
        verifying_fields,
        area.reshape(1, rows),
    )
    out, loss = pl.pallas_call(
        store,
        out_shape=(
            jax.ShapeDtypeStruct((rows, c_dim), BF16),
            jax.ShapeDtypeStruct((1, 1), F32),
        ),
        in_specs=[pl.BlockSpec(memory_space=pltpu.VMEM)] * 2,
        out_specs=(anywhere, anywhere),
        scratch_shapes=[pltpu.VMEM((1, 1), F32), dma((2,))],
        compiler_params=pltpu.CompilerParams(vmem_limit_bytes=16 << 20),
        name="store_result",
    )(out, loss)
    return (out[None], loss.reshape(()))


def solution(mesh):
    in_specs = (P("ens", "grid", None), P(None, "grid"), P(), P(), P(), P(None, "grid"), P("grid"))
    out_specs = (P("ens", "grid", None), P())
    return jax.shard_map(shards, mesh=mesh, in_specs=in_specs, out_specs=out_specs, check_vma=False)
```

time: 42.3 us -> 41.3 us (0.976)
  Pallas kernels: 41.5 us -> 40.5 us
    pallas_call x1, Pallas kernels: 1.31 us -> 0.81 us  [shards(): pl.pallas_call(store, out_shape=(jax.ShapeDtypeStruct((rows, c_dim), BF16...]
    pallas_call x1, Pallas kernels: 40.2 us -> 39.7 us  [shards(): pl.pallas_call(functools.partial(kernel, rows * lax.axis_size('grid')), o...]
where the time goes in v4:
time: 41.3 us; the launch traced here: 41.2 us
  Pallas kernels  40.5 us (98%)
  between operations  0.64 us (2%)
    pallas_call x1, Pallas kernels, shards(): pl.pallas_call(functools.partial(kernel, rows * lax.axis_size('grid')), o...  39.7 us

profile of v4, /device:TPU:1, one launch (start us, length us, event | category | flops | bytes accessed | tf_op | source)
XLA Modules:
  0.0 41.2 jit_solution(17932169023510005919)
XLA Ops:
  0.6 39.7 %crps_layer.1 = (bf16[256,1024]{1,0:T(8,128)(2,1)S(1)}, f32[1,128]{1,0:T(1,128)S(1)}) custom-call(bf16[256,1024]{1,0:T(8,128)(2,1)} %bitcast.5, s32[8,256]{1,0:T(8,128)} %nb_hbm.1, bf16[1024,1024]{1,0:T(8,128)(2,1)} %w_hbm.1, f32[1,1024]{1,0:T(1,128)} %bitcast.6, bf16[100,1024]{1,0:T(8,128)(2,1)} %proj_hbm.1, f32[100,256]{1,0:T(8,128)} %ver_hbm.1, ...), custom_call_target="tpu_custom_call" | custom-call | tf_op jit(solution)/shard_map/crps_layer/pallas_call | solution.py:438
  40.4 0.8 %store_result.1 = (bf16[256,1024]{1,0:T(8,128)(2,1)}, f32[1,1]{1,0:T(1,128)}) custom-call(bf16[256,1024]{1,0:T(8,128)(2,1)S(1)} %get-tuple-element.6.made, f32[1,128]{1,0:T(1,128)S(1)} %get-tuple-element.7.total), custom_call_target="tpu_custom_call" | custom-call | tf_op jit(solution)/shard_map/store_result/pallas_call | solution.py:508

commit v5 on v4

--- a/solution.py
+++ b/solution.py
@@ -220,6 +220,18 @@
     halo_near.start()
     pl.when(has_far)(halo_far.start)
 
+    def coded(f):
+        most = jnp.max(jnp.abs(f), axis=-1, keepdims=True)
+        power = jnp.ceil(jnp.log2(jnp.maximum(most, 1e-30)))
+        code = jnp.where(lane < lanes - 1, jnp.round(f * jnp.exp2(14.0 - power)), power)
+        return code.astype(jnp.int32).astype(jnp.int16)
+
+    def decoded(code):
+        f = code.astype(jnp.int32).astype(F32)
+        return jnp.where(lane < vars_n, f * jnp.exp2(f[:, lanes - 1 :] - 14.0), 0.0)
+
+    lane = lax.broadcasted_iota(jnp.int32, (1, lanes), 1)
+
     def forward(c, state, at, window):
         mixed = state.astype(F32) + dot(at, window, 0, 0) * (1.0 / nb.shape[0])
         centre = mixed - jnp.mean(mixed, axis=-1, keepdims=True)
@@ -236,7 +248,7 @@
         cdf = 0.5 * (1.0 + t)
         out = (state.astype(F32) + pre * cdf).astype(BF16)
         slope[here] = cdf + 0.5 * pre * (1.0 - t * t) * (k0 * (1.0 + 3 * 0.044715 * sq))
-        fld[here] = dot(out, pv[...], 1, 1).astype(BF16)
+        fld[here] = coded(dot(out, pv[...], 1, 1))
         fq[c][e] = fld[at_multiple(base[c] + x * share[c], share[c])]
 
     loads[1].wait()
@@ -290,14 +302,13 @@
 
     send_fields(1)
 
-    lane = lax.broadcasted_iota(jnp.int32, (1, lanes), 1)
     pair = 1.0 / (members * (members - 1))
 
     def score(c):
         all_of(fq[c], len(meet), fq_s.at[c], fq_r.at[c]).wait_recv()
         step = 16
         for lo in range(0, share[c], step):
-            f = [fq[c][m, lo : lo + step, :].astype(F32) for m in range(members)]
+            f = [decoded(fq[c][m, lo : lo + step, :]) for m in range(members)]
             want = tall[at_multiple(base[c] + x * share[c] + lo, step)]
             weight = want[:, lanes - 1 :]
             want = jnp.where(lane < vars_n, want, 0.0)
@@ -462,9 +473,9 @@
             pltpu.VMEM((rows, c_dim), F32),
             pltpu.VMEM((rows, lanes), F32),
             pltpu.VMEM((rows, c_dim), F32),
-            pltpu.VMEM((rows, lanes), BF16),
-            pltpu.VMEM((members, (rows - rim) // XN, lanes), BF16),
-            pltpu.VMEM((members, rim // XN, lanes), BF16),
+            pltpu.VMEM((rows, lanes), jnp.int16),
+            pltpu.VMEM((members, (rows - rim) // XN, lanes), jnp.int16),
+            pltpu.VMEM((members, rim // XN, lanes), jnp.int16),
             pltpu.VMEM((XN, (rows - rim) // XN, lanes), BF16),
             pltpu.VMEM((XN, rim // XN, lanes), BF16),
             pltpu.VMEM((rows, lanes), BF16),

time: 41.3 us -> 41.8 us (1.012)
  Pallas kernels: 40.5 us -> 41 us
where the time goes in v5:
time: 41.8 us; the launch traced here: 41.6 us
  Pallas kernels  41 us (98%)
  between operations  0.64 us (2%)
    pallas_call x1, Pallas kernels, shards(): pl.pallas_call(functools.partial(kernel, rows * lax.axis_size('grid')), o...  40.1 us

profile of v5, /device:TPU:1, one launch (start us, length us, event | category | flops | bytes accessed | tf_op | source)
XLA Modules:
  0.0 41.6 jit_solution(13339352811331588153)
XLA Ops:
  0.6 40.1 %crps_layer.1 = (bf16[256,1024]{1,0:T(8,128)(2,1)S(1)}, f32[1,128]{1,0:T(1,128)S(1)}) custom-call(bf16[256,1024]{1,0:T(8,128)(2,1)} %bitcast.5, s32[8,256]{1,0:T(8,128)} %nb_hbm.1, bf16[1024,1024]{1,0:T(8,128)(2,1)} %w_hbm.1, f32[1,1024]{1,0:T(1,128)} %bitcast.6, bf16[100,1024]{1,0:T(8,128)(2,1)} %proj_hbm.1, f32[100,256]{1,0:T(8,128)} %ver_hbm.1, ...), custom_call_target="tpu_custom_call" | custom-call | tf_op jit(solution)/shard_map/crps_layer/pallas_call | solution.py:449
  40.8 0.8 %store_result.1 = (bf16[256,1024]{1,0:T(8,128)(2,1)}, f32[1,1]{1,0:T(1,128)}) custom-call(bf16[256,1024]{1,0:T(8,128)(2,1)S(1)} %get-tuple-element.6.made, f32[1,128]{1,0:T(1,128)S(1)} %get-tuple-element.7.total), custom_call_target="tpu_custom_call" | custom-call | tf_op jit(solution)/shard_map/store_result/pallas_call | solution.py:519

commit v6 on v5

--- a/solution.py
+++ b/solution.py
@@ -111,9 +111,10 @@
 
     offsets = [d for d in range(-(ZL // 2) + 1, ZL // 2 + 1) if d]
     xy = [(dx, dy) for dx in range(XN) for dy in range(YN) if (dx, dy) != (0, 0)]
-    to_xy = [device(zh, (x + dx) % XN, zl, (y + dy) % YN, core) for dx, dy in xy]
-    zc = [(d, dc) for d in offsets for dc in range(CORES)]
-    to_zc = [at_z(d, (core + dc) % CORES) for d, dc in zc]
+    to_xyc = [device(zh, x, zl, y, 1 - core)] + [
+        device(zh, (x + dx) % XN, zl, (y + dy) % YN, (core + dc) % CORES) for dx, dy in xy for dc in range(CORES)
+    ]
+    to_z = [at_z(d, core) for d in offsets]
     other_core = device(zh, x, zl, y, 1 - core)
     to_x = [device(zh, (x + dx) % XN, zl, y, core) for dx in range(1, XN)]
     meet = [(dh, dx) for dh in range(ZH - 1, -1, -1) for dx in range(XN) if (dh, dx) != (0, 0)]
@@ -361,9 +362,9 @@
     score(0)
     send_g(0)
     score(1)
-    mine1 = x * YN + y
+    mine1 = (x * YN + y) * CORES + core
     lone[mine1] = jnp.where(lane < vars_n, jnp.sum(lacc[...], axis=0, keepdims=True), 0.0)
-    for to in to_xy:
+    for to in to_xyc:
         remote(lone.at[mine1], lone.at[mine1], l1_s, l1_r, to).start()
     send_g(1)
     per = 1.0 / nb.shape[0]
@@ -382,14 +383,14 @@
     grad_near = remote(gsend.at[0], garr.at[0], gh_s.at[0], gh_r.at[0], other_core)
     grad_near.start()
 
-    loss_one = all_of(lone, len(to_xy), l1_s, l1_r)
+    loss_one = all_of(lone, len(to_xyc), l1_s, l1_r)
     loss_one.wait_recv()
-    mine2 = zl * CORES + core
+    mine2 = zl
     acc = lone[0]
-    for i in range(1, XN * YN):
+    for i in range(1, XN * YN * CORES):
         acc = acc + lone[i]
     ltwo[mine2] = acc
-    for to in [other_core] + to_zc:
+    for to in to_z:
         remote(ltwo.at[mine2], ltwo.at[mine2], l2_s, l2_r, to).start()
 
     tot[...] = dot(at0[at_multiple(core * rim, rows), :], wide, 1, 0) * per
@@ -406,10 +407,10 @@
         remote(garr.at[1], garr.at[1], gh_s.at[1], gh_r.at[1], far).wait_recv()
         out_ref[far_rows] = (tot[far_rows] + garr[1].astype(F32)).astype(BF16)
 
-    loss_two = all_of(ltwo, 1 + len(to_zc), l2_s, l2_r)
+    loss_two = all_of(ltwo, len(to_z), l2_s, l2_r)
     loss_two.wait_recv()
     acc = ltwo[0]
-    for i in range(1, ZL * CORES):
+    for i in range(1, ZL):
         acc = acc + ltwo[i]
     loss = jnp.sum(acc, axis=-1, keepdims=True) * (1.0 / (total_points * vars_n))
     loss_ref[...] = jnp.broadcast_to(loss, loss_ref.shape)
@@ -445,7 +446,7 @@
     members = ZH * XN
     anywhere = pl.BlockSpec(memory_space=pl.ANY)
     dma = pltpu.SemaphoreType.DMA
-    n_xy, n_zc = XN * YN, ZL * CORES
+    n_xyc, n_z = XN * YN * CORES, ZL
     out, loss = pl.pallas_call(
         functools.partial(kernel, rows * lax.axis_size("grid")),
         out_shape=(
@@ -485,8 +486,8 @@
             pltpu.VMEM((2, rim, c_dim), BF16),
             pltpu.VMEM((2, rim, c_dim), BF16),
             pltpu.VMEM((8, lanes), F32),
-            pltpu.VMEM((n_xy, 1, lanes), F32),
-            pltpu.VMEM((n_zc, 1, lanes), F32),
+            pltpu.VMEM((n_xyc, 1, lanes), F32),
+            pltpu.VMEM((n_z, 1, lanes), F32),
             pltpu.SemaphoreType.REGULAR,
             pltpu.SemaphoreType.REGULAR,
             dma((7,)),

time: 41.8 us -> 41.1 us (0.983)
  Pallas kernels: 41 us -> 39.9 us
    pallas_call x1, Pallas kernels: 40.1 us -> 39 us  [shards(): pl.pallas_call(functools.partial(kernel, rows * lax.axis_size('grid')), o...]
where the time goes in v6:
time: 41.1 us; the launch traced here: 40.5 us
  Pallas kernels  39.9 us (97%)
  between operations  0.64 us (2%)
    pallas_call x1, Pallas kernels, shards(): pl.pallas_call(functools.partial(kernel, rows * lax.axis_size('grid')), o...  39 us

profile of v6, /device:TPU:1, one launch (start us, length us, event | category | flops | bytes accessed | tf_op | source)
XLA Modules:
  0.0 40.5 jit_solution(7489066001927212378)
XLA Ops:
  0.6 39.0 %crps_layer.1 = (bf16[256,1024]{1,0:T(8,128)(2,1)S(1)}, f32[1,128]{1,0:T(1,128)S(1)}) custom-call(bf16[256,1024]{1,0:T(8,128)(2,1)} %bitcast.5, s32[8,256]{1,0:T(8,128)} %nb_hbm.1, bf16[1024,1024]{1,0:T(8,128)(2,1)} %w_hbm.1, f32[1,1024]{1,0:T(1,128)} %bitcast.6, bf16[100,1024]{1,0:T(8,128)(2,1)} %proj_hbm.1, f32[100,256]{1,0:T(8,128)} %ver_hbm.1, ...), custom_call_target="tpu_custom_call" | custom-call | tf_op jit(solution)/shard_map/crps_layer/pallas_call | solution.py:450
  39.7 0.8 %store_result.1 = (bf16[256,1024]{1,0:T(8,128)(2,1)}, f32[1,1]{1,0:T(1,128)}) custom-call(bf16[256,1024]{1,0:T(8,128)(2,1)S(1)} %get-tuple-element.6.made, f32[1,128]{1,0:T(1,128)S(1)} %get-tuple-element.7.total), custom_call_target="tpu_custom_call" | custom-call | tf_op jit(solution)/shard_map/store_result/pallas_call | solution.py:520
